TPU v7x, 32 devices: a whole 2x2x4 slice. The times are simulated.
32 devices in a mesh: groups: 2 (over x), lon: 8 (over z, y), ens: 2 (over core).
Axes of the slice: x: 2, y: 2, z: 4, core: 2. Of those that a mesh axis runs over, the one named last changes fastest.
Arguments:
- inputs: bfloat16 [8, 16, 512, 512], P('ens', 'groups', 'lon'), parts along dimension 1, may hold values from -6 to 6
- layer_norm_gain: float32 [512], replicated, may hold values from 0.5 to 1.5
- w_qkv: bfloat16 [512, 1536], replicated, as said below
- w_out: bfloat16 [512, 512], replicated, may hold values from -0.25 to 0.25
- w_head: bfloat16 [512, 128], replicated, may hold values from -0.25 to 0.25
- target: float32 [16, 512, 128], P('groups', 'lon'), parts along dimension 0, may hold values from -6 to 6
Outputs:
- grad_input: bfloat16 [8, 16, 512, 512], P('ens', 'groups', 'lon'), parts along dimension 1
- grad_qkv: float32 [1024, 1536], P(('groups', 'lon')), parts along dimension 0
- grad_out: float32 [1024, 512], P(('groups', 'lon')), parts along dimension 0
- grad_head: float32 [1024, 128], P(('groups', 'lon')), parts along dimension 0
There are 2 independent parts, one for each index of `groups`. A program takes and returns all parts, laid end to end along the dimension named above; an argument that names none is the same for every part. Nothing has to cross between parts.
Inputs may be any that keep to these rules, and one draw needn't show every extreme that they name: `w_qkv`: entries are independent across rows and of order 512 ** -0.5 times a few.
All inputs are finite; a program needn't handle non-finite values.
Results may differ from a plain program's by a relative error of at most 0.019.
Values may be sent and summed in bfloat16 or wider, within the bound.
No kernel may reach another device: no remote copies, remote signals or barrier semaphores. Data moves between devices by JAX's collectives and lax.ppermute only.
A program may use at most 192 MiB of HBM per device.

v0:
```python
import jax
import jax.numpy as jnp
from jax import lax
from jax.sharding import PartitionSpec as P

HEADS = 16


eps_norm = 1e-05
smooth_width = 0.25
loss_scale = 32.0


def dot_t(left, right):
    return lax.dot_general(
        left, right, (((1,), (1,)), ((), ())), preferred_element_type=jnp.float32
    )


def dot_rows(left, right):
    return lax.dot_general(
        left, right, (((0,), (0,)), ((), ())), preferred_element_type=jnp.float32
    )


def slope(delta):
    return delta * lax.rsqrt(delta * delta + smooth_width * smooth_width)


def norm_pieces(input_float, layer_norm_gain):
    feature_mean = jnp.mean(input_float, axis=-1, keepdims=True)
    input_centered = input_float - feature_mean
    var = jnp.mean(input_centered * input_centered, axis=-1, keepdims=True)
    inverse_deviation = lax.rsqrt(var + eps_norm)
    standardized_input = input_centered * inverse_deviation
    return (
        standardized_input,
        inverse_deviation,
        (standardized_input * layer_norm_gain).astype(jnp.bfloat16),
    )


def norm_backward(normed_input_gradient, layer_norm_gain, standardized_input, inverse_deviation):
    scaled_input = normed_input_gradient.astype(jnp.float32) * layer_norm_gain
    return inverse_deviation * (
        scaled_input
        - jnp.mean(scaled_input, axis=-1, keepdims=True)
        - standardized_input * jnp.mean(scaled_input * standardized_input, axis=-1, keepdims=True)
    )


def crps_grad(pred, target):
    every = lax.all_gather(pred, "ens", axis=0, tiled=True).astype(jnp.float32)
    predf = pred.astype(jnp.float32)
    total = every.shape[0]
    pairwise = jnp.sum(slope(predf[:, None] - every[None, :]), axis=1)
    return (loss_scale / total * (slope(predf - target) - pairwise / (total - 1))).astype(
        jnp.bfloat16
    )


def outbound(field, lanes):
    members, lat, cols, chans = field.shape
    rows = lat // 8
    blocks = field.reshape(members, 8, rows, cols, chans).transpose(0, 2, 3, 1, 4)
    return blocks.reshape(lanes, members * rows * cols // lanes, 8, chans)


def gather_groups(arrived, lanes):
    spread = lanes // 8
    keys = arrived.shape[1]
    chans = arrived.shape[3]
    shaped = arrived.reshape(8, spread, keys, 8, chans).transpose(1, 2, 0, 3, 4)
    return shaped.reshape(spread * keys, 64, chans)


def return_groups(groups, lanes):
    spread = lanes // 8
    keys = groups.shape[0] // spread
    chans = groups.shape[2]
    shaped = groups.reshape(spread, keys, 8, 8, chans).transpose(2, 0, 1, 3, 4)
    return shaped.reshape(lanes, keys, 8, chans)


def inbound(arrived, members, lat, cols):
    rows = lat // 8
    chans = arrived.shape[3]
    shaped = arrived.reshape(members, rows, cols, 8, chans).transpose(0, 3, 1, 2, 4)
    return shaped.reshape(members, lat, cols, chans)


def heads_of(qkv):
    count, cells, three = qkv.shape
    width = three // 3
    parts = qkv.reshape(count, cells, 3, HEADS, width // HEADS)
    return (parts[:, :, 0], parts[:, :, 1], parts[:, :, 2])


def attend(qkv):
    query, keys, values = heads_of(qkv)
    scores = jnp.einsum(
        "gqhd,gkhd->ghqk", query, keys, preferred_element_type=jnp.float32
    ) * query.shape[-1] ** (-0.5)
    top = jnp.max(scores, axis=-1, keepdims=True)
    expo = jnp.exp(scores - top)
    probs = expo / jnp.sum(expo, axis=-1, keepdims=True)
    weights = probs.astype(jnp.bfloat16)
    out = jnp.einsum("ghqk,gkhd->gqhd", weights, values, preferred_element_type=jnp.float32)
    return (out.astype(jnp.bfloat16).reshape(qkv.shape[0], qkv.shape[1], -1), probs, weights)


def attend_back(qkv, probs, weights, grad):
    query, keys, values = heads_of(qkv)
    upstream = grad.reshape(query.shape)
    g_values = jnp.einsum(
        "ghqk,gqhd->gkhd", weights, upstream, preferred_element_type=jnp.float32
    ).astype(jnp.bfloat16)
    g_probs = jnp.einsum("gqhd,gkhd->ghqk", upstream, values, preferred_element_type=jnp.float32)
    inner = jnp.sum(probs * g_probs, axis=-1, keepdims=True)
    g_scores = (probs * (g_probs - inner) * query.shape[-1] ** (-0.5)).astype(jnp.bfloat16)
    g_query = jnp.einsum(
        "ghqk,gkhd->gqhd", g_scores, keys, preferred_element_type=jnp.float32
    ).astype(jnp.bfloat16)
    g_keys = jnp.einsum(
        "ghqk,gqhd->gkhd", g_scores, query, preferred_element_type=jnp.float32
    ).astype(jnp.bfloat16)
    return jnp.stack([g_query, g_keys, g_values], axis=2).reshape(qkv.shape)


def body(inputs, layer_norm_gain, w_qkv, w_out, w_head, target):
    members, lat, cols, width = inputs.shape
    lanes = lax.axis_size("lon")
    input_float = inputs.astype(jnp.float32)
    standardized_input, inverse_deviation, normed_input = norm_pieces(input_float, layer_norm_gain)
    normed_flat = normed_input.reshape(-1, width)
    qkv = (
        jnp.dot(normed_flat, w_qkv, preferred_element_type=jnp.float32)
        .astype(jnp.bfloat16)
        .reshape(members, lat, cols, 3 * width)
    )
    qkv_grid = gather_groups(
        lax.all_to_all(outbound(qkv, lanes), "lon", split_axis=0, concat_axis=0, tiled=True), lanes
    )
    attended_grid, probs, weights = attend(qkv_grid)
    attended = inbound(
        lax.all_to_all(
            return_groups(attended_grid, lanes), "lon", split_axis=0, concat_axis=0, tiled=True
        ),
        members,
        lat,
        cols,
    )
    attended_flat = attended.reshape(-1, width)
    block_out = (
        input_float.reshape(-1, width)
        + jnp.dot(attended_flat, w_out, preferred_element_type=jnp.float32)
    ).astype(jnp.bfloat16)
    pred = (
        jnp.dot(block_out, w_head, preferred_element_type=jnp.float32)
        .astype(jnp.bfloat16)
        .reshape(members, lat, cols, -1)
    )
    g_pred = crps_grad(pred, target)
    g_pred_flat = g_pred.reshape(-1, g_pred.shape[-1])
    g_block = dot_t(g_pred_flat, w_head).astype(jnp.bfloat16)
    g_att = dot_t(g_block, w_out).astype(jnp.bfloat16).reshape(members, lat, cols, width)
    g_att_grid = gather_groups(
        lax.all_to_all(outbound(g_att, lanes), "lon", split_axis=0, concat_axis=0, tiled=True),
        lanes,
    )
    g_qkv_grid = attend_back(qkv_grid, probs, weights, g_att_grid)
    g_qkv = inbound(
        lax.all_to_all(
            return_groups(g_qkv_grid, lanes), "lon", split_axis=0, concat_axis=0, tiled=True
        ),
        members,
        lat,
        cols,
    ).reshape(-1, 3 * width)
    normed_input_gradient = (
        dot_t(g_qkv, w_qkv).astype(jnp.bfloat16).reshape(members, lat, cols, width)
    )
    qkv_pair = (normed_flat, g_qkv)
    norm_gradient = norm_backward(
        normed_input_gradient, layer_norm_gain, standardized_input, inverse_deviation
    )
    grad_input = (
        g_block.astype(jnp.float32).reshape(members, lat, cols, width) + norm_gradient
    ).astype(jnp.bfloat16)
    pairs = (qkv_pair, (attended_flat, g_block), (block_out, g_pred_flat))
    whole = lax.psum(
        jnp.concatenate([dot_rows(left, right) for left, right in pairs], axis=1).astype(
            jnp.bfloat16
        ),
        "ens",
    ).astype(jnp.float32)
    share = lax.psum_scatter(whole, "lon", scatter_dimension=0, tiled=True)
    grad_qkv = share[:, : 3 * width]
    grad_out = share[:, 3 * width : 4 * width]
    grad_head = share[:, 4 * width :]
    return (grad_input, grad_qkv, grad_out, grad_head)


def solution(mesh):
    in_specs = (P("ens", "groups", "lon", None), P(), P(), P(), P(), P("groups", "lon", None))
    out_specs = (
        P("ens", "groups", "lon", None),
        P(("groups", "lon"), None),
        P(("groups", "lon"), None),
        P(("groups", "lon"), None),
    )
    return jax.shard_map(body, mesh=mesh, in_specs=in_specs, out_specs=out_specs, check_vma=False)
```

profile of v0, /device:TPU:0, one launch (start us, length us, event | category | flops | bytes accessed | tf_op | source)
XLA Modules:
  0.0 894.1 jit_solution(4906939389248874716)
XLA Ops:
  7.2 0.0 all-gather.2.cloned.1.call-start
  7.2 2.1 convert_reduce_fusion
  9.4 2.5 multiply_reduce_fusion.4
  11.9 0.9 multiply_convert_fusion.1
  12.8 3.6 convolution_convert_fusion
  16.4 3.5 copy.58
  20.0 145.7 %all_to_all.20 = bf16[8,32,8,1536]{3,2,1,0:T(8,128)(2,1)S(1)} all-to-all(bf16[8,32,8,1536]{3,2,1,0:T(8,128)(2,1)S(1)} %bitcast.112), channel_id=1, replica_groups=mesh['groups'=2,'lon'=8,'ens'=2] {'lon'}, dimensions={0} | all-to-all | bytes 12582912 | tf_op jit(solution)/shard_map/all_to_all | solution.py:142
  165.7 3.5 copy.59
  169.2 27.8 %reshape_reshape.26 = bf16[32,64,3,16,32]{4,3,2,1,0:T(8,128)(2,1)} reshape(bf16[1,32,8,8,1536]{4,3,2,1,0:T(8,128)(2,1)} %copy.59) | data formatting | bytes 12582912 | tf_op jit(solution)/shard_map/reshape;reshape | solution.py:95
  197.0 17.5 %fusion.54 = (bf16[32,64,1,16,32]{4,3,2,1,0:T(8,128)(2,1)}, bf16[32,64,1,16,32]{4,3,2,1,0:T(8,128)(2,1)}, bf16[32,64,1,16,32]{4,3,2,1,0:T(8,128)(2,1)}) fusion(bf16[32,64,3,16,32]{4,3,2,1,0:T(8,128)(2,1)} %reshape_reshape.26), kind=kLoop, calls=%fused_computation.69 | loop fusion | bytes 12582912 | tf_op jit(solution)/shard_map/slice | solution.py:96
  214.5 10.2 %copy.86 = bf16[32,64,1,16,32]{1,4,3,0,2:T(8,128)(2,1)} copy(bf16[32,64,1,16,32]{4,3,2,1,0:T(8,128)(2,1)} %get-tuple-element.4) | data formatting | bytes 4194304
  224.7 10.2 %copy.87 = bf16[32,64,1,16,32]{1,4,3,0,2:T(8,128)(2,1)} copy(bf16[32,64,1,16,32]{4,3,2,1,0:T(8,128)(2,1)} %get-tuple-element.6) | data formatting | bytes 4194304
  234.9 11.6 %fusion.20 = f32[32,16,64,64]{2,3,1,0:T(8,128)} fusion(bf16[32,64,1,16,32]{1,4,3,0,2:T(8,128)(2,1)} %copy.87, bf16[32,64,1,16,32]{1,4,3,0,2:T(8,128)(2,1)} %copy.86), kind=kOutput, calls=%fused_computation.22 | convolution fusion | flops 134217728 | bytes 12582912 | tf_op jit(solution)/shard_map/gqhd,gkhd->ghqk/dot_general | solution.py:101
  246.6 18.4 %fusion.55 = (f32[32,16,64]{2,1,0:T(8,128)S(1)}, f32[32,16,64,64]{2,3,1,0:T(8,128)}) fusion(f32[32,16,64,64]{2,3,1,0:T(8,128)} %fusion.20), kind=kOutput, calls=%fused_computation.70 | output fusion | flops 8388671 | bytes 16908288 | tf_op jit(solution)/shard_map/sub | solution.py:105
  264.9 10.4 %copy.85 = bf16[32,64,1,16,32]{1,4,3,0,2:T(8,128)(2,1)} copy(bf16[32,64,1,16,32]{4,3,2,1,0:T(8,128)(2,1)} %get-tuple-element.5) | data formatting | bytes 4194304
  275.3 11.3 %convert_bitcast_fusion.3 = bf16[32,64,16,32]{1,3,2,0:T(8,128)(2,1)} fusion(bf16[32,64,1,16,32]{1,4,3,0,2:T(8,128)(2,1)} %copy.85, f32[32,16,64,64]{2,3,1,0:T(8,128)} %get-tuple-element.8, f32[32,16,64]{2,1,0:T(8,128)S(1)} %get-tuple-element.7), kind=kOutput, calls=%fused_computation.37 | convolution fusion | flops 139460608 | bytes 12713984 | tf_op jit(solution)/shard_map/ghqk,gkhd->gqhd/dot_general | solution.py:108
  286.7 10.1 %copy.64 = bf16[32,64,16,32]{3,2,1,0:T(8,128)(2,1)} copy(bf16[32,64,16,32]{1,3,2,0:T(8,128)(2,1)} %convert_bitcast_fusion.3) | data formatting | bytes 4194304 | tf_op jit(solution)/shard_map/convert_element_type | solution.py:109
  296.7 12.0 %reshape_reshape.27 = bf16[1,32,8,8,512]{4,3,2,1,0:T(8,128)(2,1)} reshape(bf16[32,64,16,32]{3,2,1,0:T(8,128)(2,1)} %copy.64) | data formatting | bytes 4194304 | tf_op jit(solution)/shard_map/reshape;reshape | solution.py:81
  308.7 1.8 copy.65
  310.5 51.5 %all_to_all.21 = bf16[8,32,8,512]{3,2,1,0:T(8,128)(2,1)S(1)} all-to-all(bf16[8,32,8,512]{3,2,1,0:T(8,128)(2,1)S(1)} %copy.65), channel_id=1, replica_groups=mesh['groups'=2,'lon'=8,'ens'=2] {'lon'}, dimensions={0} | all-to-all | bytes 4194304 | tf_op jit(solution)/shard_map/all_to_all | solution.py:146
  362.0 0.7 copy.66
  362.8 1.3 fusion.28
  364.1 1.9 bitcast_convert_fusion
  366.0 8.1 all-gather.2.cloned.1.call-done
  374.1 1.5 convert_element_type.98
  375.6 2.8 fusion.10
  378.5 0.1 broadcast_multiply_fusion
  378.6 0.3 fusion.48
  378.9 0.7 convolution_convert_fusion.1
  379.6 1.3 convolution_convert_fusion.4
  380.9 0.0 copy-done.4
  381.0 1.2 copy.67
  382.1 54.2 %all_to_all.22 = bf16[8,32,8,512]{3,2,1,0:T(8,128)(2,1)S(1)} all-to-all(bf16[8,32,8,512]{3,2,1,0:T(8,128)(2,1)S(1)} %bitcast.121), channel_id=1, replica_groups=mesh['groups'=2,'lon'=8,'ens'=2] {'lon'}, dimensions={0} | all-to-all | bytes 4194304 | tf_op jit(solution)/shard_map/all_to_all | solution.py:168
  436.4 1.6 copy.68
  438.0 10.2 %reshape_reshape.30 = bf16[32,64,16,32]{3,2,1,0:T(8,128)(2,1)} reshape(bf16[1,32,8,8,512]{4,3,2,1,0:T(8,128)(2,1)} %copy.68) | data formatting | bytes 4194304 | tf_op jit(solution)/shard_map/reshape;reshape | solution.py:114
  448.2 10.2 %copy.69 = bf16[32,64,16,32]{1,3,2,0:T(8,128)(2,1)} copy(bf16[32,64,16,32]{3,2,1,0:T(8,128)(2,1)} %reshape_reshape.30) | data formatting | bytes 4194304 | tf_op jit(solution)/shard_map/reshape;reshape | solution.py:114
  458.5 11.6 %fusion.24 = f32[32,16,64,64]{2,3,1,0:T(8,128)} fusion(bf16[32,64,16,32]{1,3,2,0:T(8,128)(2,1)} %copy.69, bf16[32,64,1,16,32]{1,4,3,0,2:T(8,128)(2,1)} %copy.85), kind=kOutput, calls=%fused_computation.26 | convolution fusion | flops 134217728 | bytes 12582912 | tf_op jit(solution)/shard_map/gqhd,gkhd->ghqk/dot_general | solution.py:118
  470.1 28.1 %convert_bitcast_fusion.2 = bf16[32,64,1,16,32]{1,4,3,0,2:T(8,128)(2,1)} fusion(f32[32,16,64,64]{2,3,1,0:T(8,128)} %fusion.24, bf16[32,64,1,16,32]{1,4,3,0,2:T(8,128)(2,1)} %copy.87, f32[32,16,64,64]{2,3,1,0:T(8,128)} %get-tuple-element.8, f32[32,16,64]{2,1,0:T(8,128)S(1)} %get-tuple-element.7), kind=kOutput, calls=%fused_computation.36 | convolution fusion | flops 149979200 | bytes 21102592 | tf_op jit(solution)/shard_map/ghqk,gkhd->gqhd/dot_general | solution.py:121
  498.2 28.0 %convert_bitcast_fusion.1 = bf16[32,64,1,16,32]{1,4,3,0,2:T(8,128)(2,1)} fusion(f32[32,16,64,64]{2,3,1,0:T(8,128)} %fusion.24, bf16[32,64,1,16,32]{1,4,3,0,2:T(8,128)(2,1)} %copy.86, f32[32,16,64,64]{2,3,1,0:T(8,128)} %get-tuple-element.8, f32[32,16,64]{2,1,0:T(8,128)S(1)} %get-tuple-element.7), kind=kOutput, calls=%fused_computation.35 | convolution fusion | flops 149979200 | bytes 21102592 | tf_op jit(solution)/shard_map/ghqk,gqhd->gkhd/dot_general | solution.py:124
  526.3 10.8 %convert_bitcast_fusion = bf16[32,64,1,16,32]{1,4,3,0,2:T(8,128)(2,1)} fusion(bf16[32,64,16,32]{1,3,2,0:T(8,128)(2,1)} %copy.69, f32[32,16,64,64]{2,3,1,0:T(8,128)} %get-tuple-element.8, f32[32,16,64]{2,1,0:T(8,128)S(1)} %get-tuple-element.7), kind=kOutput, calls=%fused_computation.34 | convolution fusion | flops 139460608 | bytes 12713984 | tf_op jit(solution)/shard_map/ghqk,gqhd->gkhd/dot_general | solution.py:115
  537.0 8.8 pad_maximum_fusion
  545.8 27.5 %copy.74 = bf16[32,64,3,16,32]{4,3,2,1,0:T(8,128)(2,1)} copy(bf16[32,64,3,16,32]{1,4,3,0,2:T(8,128)(2,1)} %pad_maximum_fusion) | data formatting | bytes 12582912 | tf_op jit(solution)/shard_map/stack | solution.py:127
  573.3 32.7 %reshape_reshape.31 = bf16[1,32,8,8,1536]{4,3,2,1,0:T(8,128)(2,1)} reshape(bf16[32,64,3,16,32]{4,3,2,1,0:T(8,128)(2,1)} %copy.74) | data formatting | bytes 12582912 | tf_op jit(solution)/shard_map/reshape;reshape | solution.py:81
  606.0 6.0 copy.75
  612.1 4.8 all-to-all-start.3
  616.8 0.0 all-reduce.2.cloned.1.call-start
  616.9 2.3 convolution_convert_fusion.7
  619.3 3.5 convolution_convert_fusion.6
  622.8 131.8 %all-to-all-done.3 = bf16[8,32,8,1536]{3,2,1,0:T(8,128)(2,1)} async-done(((bf16[8,32,8,1536]{3,2,1,0:T(8,128)(2,1)}), bf16[8,32,8,1536]{3,2,1,0:T(8,128)(2,1)}, u32[]{:S(2)}, u32[]{:S(2)}) %all-to-all-start.3) | async-done | bytes 6291488 | tf_op jit(solution)/shard_map/all_to_all | solution.py:173
  754.6 5.1 copy.76
  759.7 3.5 convolution_convert_fusion.2
  763.2 1.5 pad_maximum_fusion.1
  764.8 0.0 reduce-scatter.2.cloned.1.call-start
  764.8 20.5 %all-reduce.2.cloned.1.call-done = bf16[512,2176]{1,0:T(8,128)(2,1)} async-done(((bf16[512,2176]{1,0:T(8,128)(2,1)}), bf16[512,2176]{1,0:T(8,128)(2,1)}) %all-reduce.2.cloned.1.call-update) | async-done | bytes 2228240 | tf_op jit(solution)/shard_map/psum | solution.py:191
  785.3 4.1 convert_element_type.114
  789.5 8.2 multiply_reduce_fusion.3
  797.7 0.1 div.38
  797.8 3.9 multiply_reduce_fusion.2
  801.7 0.2 copy-done.5
  801.9 4.4 fusion.18
  806.3 76.1 %reduce-scatter.2.cloned.1.call-done = f32[64,2176]{1,0:T(8,128)} async-done(((f32[512,2176]{1,0:T(8,128)}), f32[64,2176]{1,0:T(8,128)}) %reduce-scatter.2.cloned.1.call-update) | async-done | bytes 557072 | tf_op jit(solution)/shard_map/reduce_scatter | solution.py:197
  882.4 1.8 slice.30
  884.2 1.6 slice.31
  885.7 1.4 slice.32
  (53 shorter events, 0.2 us)
Async XLA Ops:
  7.2 5.6 copy-start
  7.2 4.7 copy-start.20
  7.2 366.9 %all-gather.2.cloned.1.call-start = ((), (), s32[]{:S(2)}) async-start(), calls=%async_computation.5 | async-start | bytes 1572864 | tf_op jit(solution)/shard_map/all_gather | solution.py:53
  7.2 4.6 copy-start.1
  9.4 3.4 copy-start.15
  11.9 0.9 copy-start.17
  12.8 3.6 copy-start.12
  310.5 52.3 %copy-start.2 = (bf16[4,8,64,512]{3,2,1,0:T(8,128)(2,1)S(1)}, bf16[4,8,64,512]{3,2,1,0:T(8,128)(2,1)}, u32[]{:S(2)}) copy-start(bf16[4,8,64,512]{3,2,1,0:T(8,128)(2,1)} %param.6) | copy-start | bytes 6291460
  310.5 52.3 %copy-start.22 = (bf16[512,512]{1,0:T(8,128)(2,1)S(1)}, bf16[512,512]{1,0:T(8,128)(2,1)}, u32[]{:S(2)}) copy-start(bf16[512,512]{1,0:T(8,128)(2,1)} %param.9) | copy-start | bytes 1572868
  362.8 1.3 copy-start.6
  362.8 1.3 copy-start.14
  364.1 1.9 copy-start.7
  366.0 12.5 %copy-start.9 = (bf16[2048,128]{1,0:T(8,128)(2,1)S(1)}, bf16[2048,128]{1,0:T(8,128)(2,1)}, u32[]{:S(2)}) copy-start(bf16[2048,128]{1,0:T(8,128)(2,1)} %get-tuple-element.10) | copy-start | bytes 1572868
  366.0 12.5 %copy-start.19 = (f32[8,64,128]{2,1,0:T(8,128)S(1)}, f32[8,64,128]{2,1,0:T(8,128)}, u32[]{:S(2)}) copy-start(f32[8,64,128]{2,1,0:T(8,128)} %param.11) | copy-start | bytes 786436
  378.4 1.2 copy-start.23
  379.6 1.3 copy-start.4
  526.3 10.8 %copy-start.10 = (bf16[32,64,1,16,32]{1,4,3,0,2:T(8,128)(2,1)S(1)}, bf16[32,64,1,16,32]{1,4,3,0,2:T(8,128)(2,1)}, u32[]{:S(2)}) copy-start(bf16[32,64,1,16,32]{1,4,3,0,2:T(8,128)(2,1)} %convert_bitcast_fusion.2) | copy-start | bytes 6291460
  526.3 10.8 %copy-start.11 = (bf16[32,64,1,16,32]{1,4,3,0,2:T(8,128)(2,1)S(1)}, bf16[32,64,1,16,32]{1,4,3,0,2:T(8,128)(2,1)}, u32[]{:S(2)}) copy-start(bf16[32,64,1,16,32]{1,4,3,0,2:T(8,128)(2,1)} %convert_bitcast_fusion.1) | copy-start | bytes 6291460
  612.1 142.5 %all-to-all-start.3 = ((bf16[8,32,8,1536]{3,2,1,0:T(8,128)(2,1)}), bf16[8,32,8,1536]{3,2,1,0:T(8,128)(2,1)}, u32[]{:S(2)}, u32[]{:S(2)}) async-start(bf16[8,32,8,1536]{3,2,1,0:T(8,128)(2,1)} %copy.75), calls=%async_computation.3 | async-start | bytes 12582912 | tf_op jit(solution)/shard_map/all_to_all | solution.py:173
  616.8 168.5 %all-reduce.2.cloned.1.call-start = ((), (), s32[]{:S(2)}) async-start(), calls=%async_computation.6 | async-start | bytes 4456448 | tf_op jit(solution)/shard_map/psum | solution.py:191
  754.6 5.1 copy-start.13
  759.7 3.5 copy-start.8
  764.8 24.7 %copy-start.21 = (f32[512]{0:T(512)S(1)}, f32[512]{0:T(512)}, u32[]{:S(2)}) copy-start(f32[512]{0:T(512)} %param.7) | copy-start | bytes 6148
  764.8 117.6 %reduce-scatter.2.cloned.1.call-start = ((), (), s32[]{:S(2)}) async-start(), calls=%async_computation.7 | async-start | bytes 5013504 | tf_op jit(solution)/shard_map/reduce_scatter | solution.py:197
  789.4 8.3 copy-start.16
  789.4 8.3 copy-start.18
  797.8 3.9 copy-start.3
  797.8 4.1 copy-start.5
Sparse Core Ops, SparseCore 0:
  366.1 7.9 all-gather.1
  764.9 20.4 all-reduce.1
  789.5 92.8 reduce-scatter.1
where the time goes:
time: 903 us; the launch traced here: 894 us
  blocking collectives  251 us (28%)
  waiting for transfers between devices  237 us (26%)
  local copies, waits for them, and re-layouts  207 us (23%)
  matrix products  128 us (14%)
  other arithmetic  51.2 us (6%)
  between operations  14.7 us (2%)
    all_to_all x1, blocking collectives, body(): lax.all_to_all(outbound(qkv, lanes), 'lon', split_axis=0, concat_axis=0,...  146 us
    all_to_all x1, waiting for transfers between devices, body(): lax.all_to_all(return_groups(g_qkv_grid, lanes), 'lon', split_axis=0, con...  132 us
    reduce_scatter x1, waiting for transfers between devices, body(): share = lax.psum_scatter(whole, 'lon', scatter_dimension=0, tiled=True)  76.1 us
    all_to_all x1, blocking collectives, body(): lax.all_to_all(outbound(g_att, lanes), 'lon', split_axis=0, concat_axis=0...  54.2 us
    all_to_all x1, blocking collectives, body(): lax.all_to_all(return_groups(attended_grid, lanes), 'lon', split_axis=0,...  51.5 us
    another operation x2, local copies, waits for them, and re-layouts, return_groups(): shaped = groups.reshape(spread, keys, 8, 8, chans).transpose(2, 0, 1, 3, 4)  44.7 us
    unnamed x51, local copies, waits for them, and re-layouts  31.2 us
    dot_general x1, matrix products, attend_back(): jnp.einsum('ghqk,gkhd->gqhd', g_scores, keys, preferred_element_type=jnp....  28.1 us
  transfers between devices with their start and end apart: 4, of which 4 were waited for; matrix products, arithmetic and copies ran while one was open for 3% of the time, Pallas kernels for 0%

commit v1 on v0

v1 whole, which is shorter than its diff:
```python
import functools

import jax
import jax.numpy as jnp
from jax import lax
from jax.experimental import pallas as pl
from jax.experimental.pallas import tpu as pltpu
from jax.sharding import Mesh
from jax.sharding import PartitionSpec as P

HEADS = 16
CELLS = 8
eps_norm = 1e-05
smooth_width = 0.25
loss_scale = 32.0
LOG2E = 1.4426950408889634
CHUNKS = 4

bf16 = jnp.bfloat16
f32 = jnp.float32


def dot(left, right):
    return jnp.dot(left, right, preferred_element_type=f32)


def dot_t(left, right):
    return lax.dot_general(left, right, (((1,), (1,)), ((), ())), preferred_element_type=f32)


def dot_rows(left, right):
    return lax.dot_general(left, right, (((0,), (0,)), ((), ())), preferred_element_type=f32)


def slope(delta):
    return delta * lax.rsqrt(delta * delta + smooth_width * smooth_width)


def expand(block, mask):
    return jnp.concatenate([block] * 4, axis=0) * mask


def diagonal(wide, lane, dim):
    cells = wide.shape[0] // 4
    out = wide[:cells]
    for h in range(1, 4):
        out = jnp.where(lane >= h * dim, wide[h * cells : (h + 1) * cells], out)
    return out


def block_kernel(members, width, chans, first, *refs):
    if first:
        x_ref, gain_ref, wqkv_ref, wout_ref, whead_ref, gx_ref, acc_ref = refs[:7]
        scratch = refs[7:]
        prev_ref = None
    else:
        x_ref, gain_ref, wqkv_ref, wout_ref, whead_ref, prev_ref, gx_ref, acc_ref = refs[:8]
        scratch = refs[8:]
    xf, normed, normed_t, qkv, g_qkv, att, probs, bout, g_pred, g_block, g_att, mask_ref, acc = scratch
    cells = CELLS * CELLS
    rows = members * cells
    half = members // 2
    dim = width // HEADS
    pack = 4 * dim
    packs = width // pack
    scale = dim ** (-0.5)
    step = pl.program_id(0)
    tile = 256

    @pl.when(step == 0)
    def _():
        if first:
            acc[...] = jnp.zeros_like(acc)
        else:
            acc[...] = prev_ref[...]
        row_head = lax.broadcasted_iota(jnp.int32, (4 * cells, pack), 0) // cells
        lane_head = lax.broadcasted_iota(jnp.int32, (4 * cells, pack), 1) // dim
        mask_ref[...] = jnp.where(row_head == lane_head, 1.0, 0.0).astype(bf16)

    lane = lax.broadcasted_iota(jnp.int32, (cells, pack), 1)

    for c in range(CELLS):
        for s in range(2):
            for m in range(half):
                top = (s * half + m) * cells + c * CELLS
                xf[top : top + CELLS, :] = x_ref[
                    c * 2 + s, 0, :, m * width : (m + 1) * width
                ].astype(f32)

    gain = gain_ref[...]

    @pl.loop(0, members)
    def _(m):
        at = pl.ds(pl.multiple_of(m * cells, cells), cells)
        x = xf[at, :]
        centered = x - jnp.mean(x, axis=-1, keepdims=True)
        var = jnp.mean(centered * centered, axis=-1, keepdims=True)
        normed[at, :] = (centered * lax.rsqrt(var + eps_norm) * gain).astype(bf16)

    @pl.loop(0, 3 * width // tile)
    def _(n):
        at = pl.ds(pl.multiple_of(n * tile, tile), tile)
        qkv[:, at] = dot(normed[...], wqkv_ref[:, at]).astype(bf16)

    @pl.loop(0, members)
    def _(m):
        at = pl.ds(pl.multiple_of(m * cells, cells), cells)
        mask = mask_ref[...]
        for p in range(packs):
            q = qkv[at, p * pack : (p + 1) * pack]
            k = qkv[at, width + p * pack : width + (p + 1) * pack]
            v = qkv[at, 2 * width + p * pack : 2 * width + (p + 1) * pack]
            scores = dot_t(k, expand(q, mask))
            top = jnp.max(scores, axis=0, keepdims=True)
            expo = jnp.exp2((scores - top) * (scale * LOG2E))
            prob = expo * (1.0 / jnp.sum(expo, axis=0, keepdims=True))
            probs[m, p] = prob
            out = dot_rows(prob.astype(bf16), v)
            att[at, p * pack : (p + 1) * pack] = diagonal(out, lane, dim).astype(bf16)

    bout[...] = (xf[...] + dot(att[...], wout_ref[...])).astype(bf16)
    pred = dot(bout[...], whead_ref[...]).astype(bf16).astype(f32).reshape(members, cells, chans)
    parts = []
    for c in range(CELLS):
        high = x_ref[c * 2, 0, :, half * width :].astype(f32)
        low = x_ref[c * 2 + 1, 0, :, half * width :].astype(f32)
        parts.append(high + low)
    target = jnp.concatenate(parts, axis=0)
    pair = [jnp.zeros((cells, chans), f32) for _ in range(members)]
    for a in range(members):
        for b in range(a + 1, members):
            s = slope(pred[a] - pred[b])
            pair[a] = pair[a] + s
            pair[b] = pair[b] - s
    for a in range(members):
        g_pred[a * cells : (a + 1) * cells, :] = (
            loss_scale / members * (slope(pred[a] - target) - pair[a] / (members - 1))
        ).astype(bf16)
    g_block[...] = dot_t(g_pred[...], whead_ref[...]).astype(bf16)
    g_att[...] = dot_t(g_block[...], wout_ref[...]).astype(bf16)

    @pl.loop(0, members)
    def _(m):
        at = pl.ds(pl.multiple_of(m * cells, cells), cells)
        mask = mask_ref[...]
        for p in range(packs):
            q = qkv[at, p * pack : (p + 1) * pack]
            k = qkv[at, width + p * pack : width + (p + 1) * pack]
            v = qkv[at, 2 * width + p * pack : 2 * width + (p + 1) * pack]
            upstream = expand(g_att[at, p * pack : (p + 1) * pack], mask)
            prob = probs[m, p]
            g_prob = dot_t(v, upstream)
            inner = jnp.sum(prob * g_prob, axis=0, keepdims=True)
            g_score = (prob * (g_prob - inner) * scale).astype(bf16)
            g_q = diagonal(dot_rows(g_score, k), lane, dim)
            g_k = dot(g_score, expand(q, mask))
            g_v = dot(prob.astype(bf16), upstream)
            g_qkv[at, p * pack : (p + 1) * pack] = g_q.astype(bf16)
            g_qkv[at, width + p * pack : width + (p + 1) * pack] = g_k.astype(bf16)
            g_qkv[at, 2 * width + p * pack : 2 * width + (p + 1) * pack] = g_v.astype(bf16)

    normed_t[...] = normed[...].T

    @pl.loop(0, 3 * width // tile)
    def _(n):
        at = pl.ds(pl.multiple_of(n * tile, tile), tile)
        acc[:, at] += dot(normed_t[...], g_qkv[:, at])

    normed_t[...] = att[...].T

    @pl.loop(0, width // tile)
    def _(n):
        at = pl.ds(pl.multiple_of(n * tile, tile), tile)
        there = pl.ds(pl.multiple_of(3 * width + n * tile, tile), tile)
        acc[:, there] += dot(normed_t[...], g_block[:, at])

    acc[:, 4 * width :] += dot_rows(bout[...], g_pred[...])

    @pl.loop(0, width // tile)
    def _(n):
        at = pl.ds(pl.multiple_of(n * tile, tile), tile)
        g_att[:, at] = dot_t(g_qkv[...], wqkv_ref[at, :]).astype(bf16)

    for m in range(members):
        x = xf[m * cells : (m + 1) * cells, :]
        centered = x - jnp.mean(x, axis=-1, keepdims=True)
        var = jnp.mean(centered * centered, axis=-1, keepdims=True)
        rstd = lax.rsqrt(var + eps_norm)
        xhat = centered * rstd
        h = g_att[m * cells : (m + 1) * cells, :].astype(f32) * gain
        grad = rstd * (
            h
            - jnp.mean(h, axis=-1, keepdims=True)
            - xhat * jnp.mean(h * xhat, axis=-1, keepdims=True)
        )
        grad = grad + g_block[m * cells : (m + 1) * cells, :].astype(f32)
        s, mm = m // half, m % half
        for c in range(CELLS):
            gx_ref[c * 2 + s, 0, :, mm * width : (mm + 1) * width] = grad[
                c * CELLS : (c + 1) * CELLS, :
            ].astype(bf16)

    @pl.when(step == pl.num_programs(0) - 1)
    def _():
        acc_ref[...] = acc[...].astype(acc_ref.dtype)


def block_call(x, gain, w_qkv, w_out, w_head, prev, last):
    sources, count, lat, lanes = x.shape
    width, chans = w_head.shape
    members = 2 * ((lanes - chans) // width)
    rows = members * CELLS * CELLS
    total = 4 * width + chans
    whole = lambda shape: pl.BlockSpec(shape, lambda i: (0,) * len(shape))
    in_specs = [
        pl.BlockSpec((sources, 1, lat, lanes), lambda i: (0, i, 0, 0)),
        whole((1, width)),
        whole(w_qkv.shape),
        whole(w_out.shape),
        whole(w_head.shape),
    ]
    args = [x, gain, w_qkv, w_out, w_head]
    if prev is not None:
        in_specs.append(whole((width, total)))
        args.append(prev)
    cells = CELLS * CELLS
    pack = 4 * (width // HEADS)
    return pl.pallas_call(
        functools.partial(block_kernel, members, width, chans, prev is None),
        grid=(count,),
        in_specs=in_specs,
        out_specs=[
            pl.BlockSpec((sources, 1, lat, lanes - chans), lambda i: (0, i, 0, 0)),
            whole((width, total)),
        ],
        out_shape=[
            jax.ShapeDtypeStruct((sources, count, lat, lanes - chans), bf16),
            jax.ShapeDtypeStruct((width, total), bf16 if last else f32),
        ],
        scratch_shapes=[
            pltpu.VMEM((rows, width), f32),
            pltpu.VMEM((rows, width), bf16),
            pltpu.VMEM((rows, width), bf16),
            pltpu.VMEM((rows, 3 * width), bf16),
            pltpu.VMEM((rows, 3 * width), bf16),
            pltpu.VMEM((rows, width), bf16),
            pltpu.VMEM((members, width // pack, cells, 4 * cells), f32),
            pltpu.VMEM((rows, width), bf16),
            pltpu.VMEM((rows, chans), bf16),
            pltpu.VMEM((rows, width), bf16),
            pltpu.VMEM((rows, width), bf16),
            pltpu.VMEM((4 * cells, pack), bf16),
            pltpu.VMEM((width, total), f32),
        ],
        compiler_params=pltpu.CompilerParams(vmem_limit_bytes=48 * 1024 * 1024),
        cost_estimate=pl.CostEstimate(
            flops=count * 8_000_000_000, bytes_accessed=16_000_000, transcendentals=1_000_000
        ),
        name="grid_block",
    )(*args)


def body(inputs, layer_norm_gain, w_qkv, w_out, w_head, target):
    members, lat, cols, width = inputs.shape
    chans = target.shape[-1]
    axes = ("col", "ens")
    owners = lax.axis_size("col") * lax.axis_size("ens")
    each = cols // owners
    gain = layer_norm_gain.reshape(1, width)
    high = lax.reduce_precision(target, 8, 7)
    target_part = jnp.where(lax.axis_index("ens") == 0, high, target - high).astype(bf16)
    send_x = inputs.reshape(members, lat, each, owners, width).transpose(2, 3, 1, 0, 4)
    send_x = send_x.reshape(each, owners, lat, members * width)
    send_t = target_part.reshape(lat, each, owners, chans).transpose(1, 2, 0, 3)
    send = jnp.concatenate([send_x, send_t], axis=-1)

    per = each // CHUNKS
    arrived = []
    for j in range(CHUNKS):
        part = send[j * per : (j + 1) * per].transpose(1, 0, 2, 3)
        arrived.append(lax.all_to_all(part, axes, split_axis=0, concat_axis=0, tiled=True))
    acc = None
    grads = []
    for j in range(CHUNKS):
        g, acc = block_call(arrived[j], gain, w_qkv, w_out, w_head, acc, j == CHUNKS - 1)
        grads.append(lax.all_to_all(g, axes, split_axis=0, concat_axis=0, tiled=True))
    grad = jnp.concatenate([g.transpose(1, 0, 2, 3) for g in grads], axis=0)
    grad_input = (
        grad.reshape(each, owners, lat, members, width)
        .transpose(3, 2, 0, 1, 4)
        .reshape(members, lat, cols, width)
    )
    share = lax.psum_scatter(acc, ("col", "spread"), scatter_dimension=0, tiled=True)
    share = lax.psum(share, "ens").astype(f32)
    grad_qkv = share[:, : 3 * width]
    grad_out = share[:, 3 * width : 4 * width]
    grad_head = share[:, 4 * width :]
    return (grad_input, grad_qkv, grad_out, grad_head)


def solution(mesh):
    groups, lon, ens = mesh.devices.shape
    split = Mesh(
        mesh.devices.reshape(groups, CELLS, lon // CELLS, ens), ("groups", "col", "spread", "ens")
    )
    lon_axes = ("col", "spread")
    in_specs = (
        P("ens", "groups", lon_axes, None),
        P(),
        P(),
        P(),
        P(),
        P("groups", lon_axes, None),
    )
    rows = P(("groups",) + lon_axes, None)
    out_specs = (P("ens", "groups", lon_axes, None), rows, rows, rows)
    return jax.shard_map(body, mesh=split, in_specs=in_specs, out_specs=out_specs, check_vma=False)
```

time: 903 us -> 296 us (0.33)
  waiting for transfers between devices: 237 us -> 22.4 us
  local copies, waits for them, and re-layouts: 207 us -> 14.1 us
  blocking collectives: 251 us -> 113 us
  matrix products: 128 us -> 0 us
  Pallas kernels: 0 us -> 112 us
  other arithmetic: 51.2 us -> 2.46 us
  starting transfers between devices: 4.87 us -> 16.7 us
    all_to_all x3 -> x5, blocking collectives: 251 us -> 113 us  [the longest x3 69.9 us: body(): lax.all_to_all(g, axes, split_axis=0, concat_axis=0, tiled=True)]
    dot_general x15 -> x0, matrix products: 128 us -> none  [the longest x1 28.1 us: attend_back(): jnp.einsum('ghqk,gkhd->gqhd', g_scores, keys, preferred_element_type=jnp....]
    another operation x8 -> x0, local copies, waits for them, and re-layouts: 125 us -> none  [the longest x2 44.7 us: return_groups(): shaped = groups.reshape(spread, keys, 8, 8, chans).transpose(2, 0, 1, 3, 4)]
    all_to_all x1 -> x3, waiting for transfers between devices: 132 us -> 9.65 us  [the longest x1 9.64 us: body(): lax.all_to_all(g, axes, split_axis=0, concat_axis=0, tiled=True)]
    pallas_call x0 -> x4, Pallas kernels: none -> 112 us  [block_call(): pl.pallas_call(functools.partial(block_kernel, members, width, chans, pre...]
    reduce_scatter x1, waiting for transfers between devices: 76.1 us -> 4.73 us  [body(): lax.psum_scatter(acc, ('col', 'spread'), scatter_dimension=0, tiled=True)]
    unnamed x51 -> x12, local copies, waits for them, and re-layouts: 31.2 us -> 4.23 us
    sub x1 -> x0, other arithmetic: 18.4 us -> none  [attend(): expo = jnp.exp(scores - top)]
  transfers between devices with their start and end apart: 4 -> 5, of which waited for: 4 -> 3; matrix products, arithmetic and copies ran while one was open for 3% -> 1% of each run, Pallas kernels for 0% -> 28%
where the time goes in v1:
time: 296 us; the launch traced here: 295 us
  blocking collectives  113 us (38%)
  Pallas kernels  112 us (38%)
  waiting for transfers between devices  22.4 us (8%)
  starting transfers between devices  16.7 us (6%)
  local copies, waits for them, and re-layouts  14.1 us (5%)
  between operations  14.1 us (5%)
    pallas_call x4, Pallas kernels, block_call(): pl.pallas_call(functools.partial(block_kernel, members, width, chans, pre...  112 us
    all_to_all x3, blocking collectives, body(): lax.all_to_all(g, axes, split_axis=0, concat_axis=0, tiled=True)  69.9 us
    all_to_all x2, blocking collectives, body(): lax.all_to_all(part, axes, split_axis=0, concat_axis=0, tiled=True)  43.5 us
    all_to_all x1, waiting for transfers between devices, body(): lax.all_to_all(g, axes, split_axis=0, concat_axis=0, tiled=True)  9.64 us
    all_to_all x2, starting transfers between devices, body(): lax.all_to_all(part, axes, split_axis=0, concat_axis=0, tiled=True)  9.54 us
    psum x1, waiting for transfers between devices, body(): share = lax.psum(share, 'ens').astype(f32)  7.97 us
    all_to_all x1, starting transfers between devices, body(): lax.all_to_all(g, axes, split_axis=0, concat_axis=0, tiled=True)  7.1 us
  transfers between devices with their start and end apart: 5, of which 3 were waited for; matrix products, arithmetic and copies ran while one was open for 1% of the time, Pallas kernels for 28%

profile of v1, /device:TPU:0, one launch (start us, length us, event | category | flops | bytes accessed | tf_op | source)
XLA Modules:
  0.0 295.4 jit_solution(14962176615478084955)
XLA Ops:
  7.2 1.0 fusion.7
  8.2 0.1 copy.17
  8.3 2.8 copy.16
  11.0 1.2 fusion.3
  12.2 0.0 copy-start.3
  12.2 0.0 copy-start.4
  12.2 0.0 copy-start.5
  12.2 24.0 %all_to_all.40.refs_0_ = bf16[16,1,8,2176]{3,2,1,0:T(8,128)(2,1)S(1)} all-to-all(bf16[16,1,8,2176]{3,2,1,0:T(8,128)(2,1)S(1)} %get-tuple-element.20), channel_id=1, replica_groups=mesh['groups'=2,'lon'=8,'ens'=2] {'lon','ens'}, dimensions={0} | all-to-all | bytes 1114112 | tf_op jit(solution)/shard_map/all_to_all | solution.py:281
  36.3 19.4 %all_to_all.41.refs_0_ = bf16[16,1,8,2176]{3,2,1,0:T(8,128)(2,1)S(1)} all-to-all(bf16[16,1,8,2176]{3,2,1,0:T(8,128)(2,1)S(1)} %get-tuple-element.21), channel_id=1, replica_groups=mesh['groups'=2,'lon'=8,'ens'=2] {'lon','ens'}, dimensions={0} | all-to-all | bytes 1114112 | tf_op jit(solution)/shard_map/all_to_all | solution.py:281
  55.7 3.6 %all-to-all-start.4 = ((bf16[16,1,8,2176]{3,2,1,0:T(8,128)(2,1)}), bf16[16,1,8,2176]{3,2,1,0:T(8,128)(2,1)S(1)}, u32[]{:S(2)}, u32[]{:S(2)}) async-start(bf16[16,1,8,2176]{3,2,1,0:T(8,128)(2,1)} %get-tuple-element.23), calls=%async_computation.4 | async-start | bytes 1114112 | tf_op jit(solution)/shard_map/all_to_all | solution.py:281
  59.3 0.0 copy-done.3
  59.3 0.0 copy-done.4
  59.3 0.0 copy-done.5
  59.3 0.0 copy-start
  59.4 1.4 copy-done
  60.8 26.4 %grid_block.4 = (bf16[16,1,8,2048]{3,2,1,0:T(8,128)(2,1)S(1)}, f32[512,2176]{1,0:T(8,128)}) custom-call(bf16[16,1,8,2176]{3,2,1,0:T(8,128)(2,1)S(1)} %all_to_all.40.refs_0_, f32[1,512]{1,0:T(1,128)S(1)} %bitcast.29, bf16[512,1536]{1,0:T(8,128)(2,1)S(1)} %copy-done, bf16[512,512]{1,0:T(8,128)(2,1)S(1)} %copy-done.3, bf16[512,128]{1,0:T(8,128)(2,1)S(1)} %copy-done.4), custom_call_target="tpu_custom_call" | custom-call | flops 8000000000 | bytes 16000000 | tf_op jit(solution)/shard_map/grid_block/pallas_call | solution.py:228
  87.2 0.0 all-to-all-done.4.refs_0_
  87.2 6.0 %all-to-all-start.6 = ((bf16[16,1,8,2176]{3,2,1,0:T(8,128)(2,1)}), bf16[16,1,8,2176]{3,2,1,0:T(8,128)(2,1)S(1)}, u32[]{:S(2)}, u32[]{:S(2)}) async-start(bf16[16,1,8,2176]{3,2,1,0:T(8,128)(2,1)} %get-tuple-element.22), calls=%async_computation.6 | async-start | bytes 1114112 | tf_op jit(solution)/shard_map/all_to_all | solution.py:281
  93.1 0.0 reduce-scatter.2.cloned.1.call-start
  93.2 0.0 copy-start.1
  93.2 1.4 copy-done.1
  94.6 28.9 %grid_block.5 = (bf16[16,1,8,2048]{3,2,1,0:T(8,128)(2,1)S(1)}, f32[512,2176]{1,0:T(8,128)}) custom-call(bf16[16,1,8,2176]{3,2,1,0:T(8,128)(2,1)S(1)} %all_to_all.41.refs_0_, f32[1,512]{1,0:T(1,128)S(1)} %bitcast.30, bf16[512,1536]{1,0:T(8,128)(2,1)S(1)} %copy-done.1, bf16[512,512]{1,0:T(8,128)(2,1)S(1)} %copy-done.3, bf16[512,128]{1,0:T(8,128)(2,1)S(1)} %copy-done.4, ...), custom_call_target="tpu_custom_call" | custom-call | flops 8000000000 | bytes 16000000 | tf_op jit(solution)/shard_map/grid_block/pallas_call | solution.py:228
  123.5 28.7 %grid_block.6 = (bf16[16,1,8,2048]{3,2,1,0:T(8,128)(2,1)S(1)}, f32[512,2176]{1,0:T(8,128)}) custom-call(bf16[16,1,8,2176]{3,2,1,0:T(8,128)(2,1)S(1)} %all-to-all-done.4.refs_0_, f32[1,512]{1,0:T(1,128)S(1)} %bitcast.31, bf16[512,1536]{1,0:T(8,128)(2,1)S(1)} %copy-done.1, bf16[512,512]{1,0:T(8,128)(2,1)S(1)} %copy-done.3, bf16[512,128]{1,0:T(8,128)(2,1)S(1)} %copy-done.4, ...), custom_call_target="tpu_custom_call" | custom-call | flops 8000000000 | bytes 16000000 | tf_op jit(solution)/shard_map/grid_block/pallas_call | solution.py:228
  152.2 0.0 all-to-all-done.6.refs_0_
  152.2 0.0 copy-start.2
  152.2 1.4 copy-done.2
  153.6 28.2 %grid_block.7 = (bf16[16,1,8,2048]{3,2,1,0:T(8,128)(2,1)}, bf16[512,2176]{1,0:T(8,128)(2,1)}) custom-call(bf16[16,1,8,2176]{3,2,1,0:T(8,128)(2,1)S(1)} %all-to-all-done.6.refs_0_, f32[1,512]{1,0:T(1,128)S(1)} %bitcast.32, bf16[512,1536]{1,0:T(8,128)(2,1)S(1)} %copy-done.2, bf16[512,512]{1,0:T(8,128)(2,1)S(1)} %copy-done.3, bf16[512,128]{1,0:T(8,128)(2,1)S(1)} %copy-done.4, ...), custom_call_target="tpu_custom_call" | custom-call | flops 8000000000 | bytes 16000000 | tf_op jit(solution)/shard_map/grid_block/pallas_call | solution.py:228
  181.8 0.0 reduce-scatter.2.cloned.1.call-update
  181.8 26.8 %all_to_all.42 = bf16[16,1,8,2048]{3,2,1,0:T(8,128)(2,1)S(1)} all-to-all(bf16[16,1,8,2048]{3,2,1,0:T(8,128)(2,1)S(1)} %get-tuple-element.12), channel_id=1, replica_groups=mesh['groups'=2,'lon'=8,'ens'=2] {'lon','ens'}, dimensions={0} | all-to-all | bytes 1048576 | tf_op jit(solution)/shard_map/all_to_all | solution.py:286
  208.7 23.3 %all_to_all.43 = bf16[16,1,8,2048]{3,2,1,0:T(8,128)(2,1)S(1)} all-to-all(bf16[16,1,8,2048]{3,2,1,0:T(8,128)(2,1)S(1)} %get-tuple-element.14), channel_id=1, replica_groups=mesh['groups'=2,'lon'=8,'ens'=2] {'lon','ens'}, dimensions={0} | all-to-all | bytes 1048576 | tf_op jit(solution)/shard_map/all_to_all | solution.py:286
  232.0 19.7 %all_to_all.44 = bf16[16,1,8,2048]{3,2,1,0:T(8,128)(2,1)S(1)} all-to-all(bf16[16,1,8,2048]{3,2,1,0:T(8,128)(2,1)S(1)} %get-tuple-element.16), channel_id=1, replica_groups=mesh['groups'=2,'lon'=8,'ens'=2] {'lon','ens'}, dimensions={0} | all-to-all | bytes 1048576 | tf_op jit(solution)/shard_map/all_to_all | solution.py:286
  251.7 7.1 %all-to-all-start.7 = ((bf16[16,1,8,2048]{3,2,1,0:T(8,128)(2,1)}), bf16[16,1,8,2048]{3,2,1,0:T(8,128)(2,1)S(1)}, u32[]{:S(2)}, u32[]{:S(2)}) async-start(bf16[16,1,8,2048]{3,2,1,0:T(8,128)(2,1)} %get-tuple-element.18), calls=%async_computation.7 | async-start | bytes 1048576 | tf_op jit(solution)/shard_map/all_to_all | solution.py:286
  258.8 0.0 all-reduce.2.cloned.1.call-start
  258.9 4.7 %reduce-scatter.2.cloned.1.call-done = bf16[64,2176]{1,0:T(8,128)(2,1)} async-done(((bf16[512,2176]{1,0:T(8,128)(2,1)}), bf16[64,2176]{1,0:T(8,128)(2,1)}) %reduce-scatter.2.cloned.1.call-update) | async-done | bytes 278544 | tf_op jit(solution)/shard_map/reduce_scatter | solution.py:293
  263.6 0.0 all-reduce.2.cloned.1.call-update
  263.6 9.6 %all-to-all-done.7 = bf16[16,1,8,2048]{3,2,1,0:T(8,128)(2,1)S(1)} async-done(((bf16[16,1,8,2048]{3,2,1,0:T(8,128)(2,1)}), bf16[16,1,8,2048]{3,2,1,0:T(8,128)(2,1)S(1)}, u32[]{:S(2)}, u32[]{:S(2)}) %all-to-all-start.7) | async-done | bytes 524320 | tf_op jit(solution)/shard_map/all_to_all | solution.py:286
  273.3 0.3 maximum_bitcast_fusion
  273.5 2.5 copy.21
  276.0 8.0 %all-reduce.2.cloned.1.call-done = bf16[64,2176]{1,0:T(8,128)(2,1)} async-done(((bf16[64,2176]{1,0:T(8,128)(2,1)}), bf16[64,2176]{1,0:T(8,128)(2,1)}) %all-reduce.2.cloned.1.call-update) | async-done | bytes 278544 | tf_op jit(solution)/shard_map/psum | solution.py:294
  284.0 1.4 slice.36
  285.3 1.5 slice.35
  286.8 1.7 slice.34
Async XLA Ops:
  12.2 47.1 %copy-start.3 = (bf16[512,512]{1,0:T(8,128)(2,1)S(1)}, bf16[512,512]{1,0:T(8,128)(2,1)}, u32[]{:S(2)}) copy-start(bf16[512,512]{1,0:T(8,128)(2,1)} %refs_3_.7) | copy-start | bytes 1572868
  12.2 47.1 %copy-start.4 = (bf16[512,128]{1,0:T(8,128)(2,1)S(1)}, bf16[512,128]{1,0:T(8,128)(2,1)}, u32[]{:S(2)}) copy-start(bf16[512,128]{1,0:T(8,128)(2,1)} %refs_4_.7) | copy-start | bytes 393220
  12.2 47.1 %copy-start.5 = (f32[512]{0:T(512)S(1)}, f32[512]{0:T(512)}, u32[]{:S(2)}) copy-start(f32[512]{0:T(512)} %param.7) | copy-start | bytes 6148
  55.7 31.4 %all-to-all-start.4 = ((bf16[16,1,8,2176]{3,2,1,0:T(8,128)(2,1)}), bf16[16,1,8,2176]{3,2,1,0:T(8,128)(2,1)S(1)}, u32[]{:S(2)}, u32[]{:S(2)}) async-start(bf16[16,1,8,2176]{3,2,1,0:T(8,128)(2,1)} %get-tuple-element.23), calls=%async_computation.4 | async-start | bytes 1114112 | tf_op jit(solution)/shard_map/all_to_all | solution.py:281
  59.3 1.4 copy-start
  87.2 65.0 %all-to-all-start.6 = ((bf16[16,1,8,2176]{3,2,1,0:T(8,128)(2,1)}), bf16[16,1,8,2176]{3,2,1,0:T(8,128)(2,1)S(1)}, u32[]{:S(2)}, u32[]{:S(2)}) async-start(bf16[16,1,8,2176]{3,2,1,0:T(8,128)(2,1)} %get-tuple-element.22), calls=%async_computation.6 | async-start | bytes 1114112 | tf_op jit(solution)/shard_map/all_to_all | solution.py:281
  93.1 170.5 %reduce-scatter.2.cloned.1.call-start = ((), (), s32[]{:S(2)}) async-start(), calls=%async_computation.9 | async-start | bytes 2506752 | tf_op jit(solution)/shard_map/reduce_scatter | solution.py:293
  93.2 1.4 copy-start.1
  152.2 1.4 copy-start.2
  251.7 21.5 %all-to-all-start.7 = ((bf16[16,1,8,2048]{3,2,1,0:T(8,128)(2,1)}), bf16[16,1,8,2048]{3,2,1,0:T(8,128)(2,1)S(1)}, u32[]{:S(2)}, u32[]{:S(2)}) async-start(bf16[16,1,8,2048]{3,2,1,0:T(8,128)(2,1)} %get-tuple-element.18), calls=%async_computation.7 | async-start | bytes 1048576 | tf_op jit(solution)/shard_map/all_to_all | solution.py:286
  258.8 25.2 %all-reduce.2.cloned.1.call-start = ((), (), s32[]{:S(2)}) async-start(), calls=%async_computation.10 | async-start | bytes 557056 | tf_op jit(solution)/shard_map/psum | solution.py:294
Sparse Core Ops, SparseCore 0:
  181.9 81.6 reduce-scatter.1
  265.9 18.0 all-reduce.1

commit v2 on v1

--- a/solution.py
+++ b/solution.py
@@ -14,7 +14,7 @@
 smooth_width = 0.25
 loss_scale = 32.0
 LOG2E = 1.4426950408889634
-CHUNKS = 4
+CHUNKS = 2
 
 bf16 = jnp.bfloat16
 f32 = jnp.float32
@@ -102,21 +102,22 @@
         at = pl.ds(pl.multiple_of(n * tile, tile), tile)
         qkv[:, at] = dot(normed[...], wqkv_ref[:, at]).astype(bf16)
 
-    @pl.loop(0, members)
+    @pl.loop(0, members, unroll=8)
     def _(m):
         at = pl.ds(pl.multiple_of(m * cells, cells), cells)
         mask = mask_ref[...]
-        for p in range(packs):
-            q = qkv[at, p * pack : (p + 1) * pack]
-            k = qkv[at, width + p * pack : width + (p + 1) * pack]
-            v = qkv[at, 2 * width + p * pack : 2 * width + (p + 1) * pack]
-            scores = dot_t(k, expand(q, mask))
-            top = jnp.max(scores, axis=0, keepdims=True)
-            expo = jnp.exp2((scores - top) * (scale * LOG2E))
-            prob = expo * (1.0 / jnp.sum(expo, axis=0, keepdims=True))
-            probs[m, p] = prob
-            out = dot_rows(prob.astype(bf16), v)
-            att[at, p * pack : (p + 1) * pack] = diagonal(out, lane, dim).astype(bf16)
+        each = range(packs)
+        part = lambda p, i: qkv[at, i * width + p * pack : i * width + (p + 1) * pack]
+        scores = [dot_t(part(p, 1), expand(part(p, 0), mask)) for p in each]
+        expos = [
+            jnp.exp2((s - jnp.max(s, axis=0, keepdims=True)) * (scale * LOG2E)) for s in scores
+        ]
+        weights = [e * (1.0 / jnp.sum(e, axis=0, keepdims=True)) for e in expos]
+        for p in each:
+            probs[m, p] = weights[p]
+        outs = [dot_rows(weights[p].astype(bf16), part(p, 2)) for p in each]
+        for p in each:
+            att[at, p * pack : (p + 1) * pack] = diagonal(outs[p], lane, dim).astype(bf16)
 
     bout[...] = (xf[...] + dot(att[...], wout_ref[...])).astype(bf16)
     pred = dot(bout[...], whead_ref[...]).astype(bf16).astype(f32).reshape(members, cells, chans)
@@ -139,25 +140,27 @@
     g_block[...] = dot_t(g_pred[...], whead_ref[...]).astype(bf16)
     g_att[...] = dot_t(g_block[...], wout_ref[...]).astype(bf16)
 
-    @pl.loop(0, members)
+    @pl.loop(0, members, unroll=8)
     def _(m):
         at = pl.ds(pl.multiple_of(m * cells, cells), cells)
         mask = mask_ref[...]
-        for p in range(packs):
-            q = qkv[at, p * pack : (p + 1) * pack]
-            k = qkv[at, width + p * pack : width + (p + 1) * pack]
-            v = qkv[at, 2 * width + p * pack : 2 * width + (p + 1) * pack]
-            upstream = expand(g_att[at, p * pack : (p + 1) * pack], mask)
+        each = range(packs)
+        part = lambda p, i: qkv[at, i * width + p * pack : i * width + (p + 1) * pack]
+        ups = [expand(g_att[at, p * pack : (p + 1) * pack], mask) for p in each]
+        g_probs = [dot_t(part(p, 2), ups[p]) for p in each]
+        g_vs = [dot(probs[m, p].astype(bf16), ups[p]) for p in each]
+        g_scores = []
+        for p in each:
             prob = probs[m, p]
-            g_prob = dot_t(v, upstream)
-            inner = jnp.sum(prob * g_prob, axis=0, keepdims=True)
-            g_score = (prob * (g_prob - inner) * scale).astype(bf16)
-            g_q = diagonal(dot_rows(g_score, k), lane, dim)
-            g_k = dot(g_score, expand(q, mask))
-            g_v = dot(prob.astype(bf16), upstream)
-            g_qkv[at, p * pack : (p + 1) * pack] = g_q.astype(bf16)
-            g_qkv[at, width + p * pack : width + (p + 1) * pack] = g_k.astype(bf16)
-            g_qkv[at, 2 * width + p * pack : 2 * width + (p + 1) * pack] = g_v.astype(bf16)
+            inner = jnp.sum(prob * g_probs[p], axis=0, keepdims=True)
+            g_scores.append((prob * (g_probs[p] - inner) * scale).astype(bf16))
+        g_qs = [dot_rows(g_scores[p], part(p, 1)) for p in each]
+        g_ks = [dot(g_scores[p], expand(part(p, 0), mask)) for p in each]
+        for p in each:
+            at_p = lambda i: pl.ds(i * width + p * pack, pack)
+            g_qkv[at, at_p(0)] = diagonal(g_qs[p], lane, dim).astype(bf16)
+            g_qkv[at, at_p(1)] = g_ks[p].astype(bf16)
+            g_qkv[at, at_p(2)] = g_vs[p].astype(bf16)
 
     normed_t[...] = normed[...].T
 
@@ -260,6 +263,37 @@
     )(*args)
 
 
+def swap_halves(pair, axes, bit, keep_first):
+    count = 1
+    for axis in axes:
+        count *= lax.axis_size(axis)
+    swap = [(i, i ^ bit) for i in range(count)]
+    sent = lax.ppermute(jnp.where(keep_first, pair[1], pair[0]), axes, swap)
+    kept = jnp.where(keep_first, pair[0], pair[1])
+    return (kept.astype(f32) + sent.astype(f32)).astype(pair.dtype)
+
+
+def reduce_rows(grad):
+    lon = ("col", "spread")
+    shards = lax.axis_size("col") * lax.axis_size("spread")
+    me = lax.axis_index(lon)
+    first = lax.axis_index("ens") == 0
+    block = grad.shape[0] // shards
+    rest = grad.reshape(shards, 2, block // 2, -1).transpose(1, 0, 2, 3)
+    rest = swap_halves(rest, ("ens",), 1, first)
+    bit = 1
+    while bit < shards:
+        left = rest.shape[0]
+        pair = rest.reshape(left // 2, 2, *rest.shape[1:]).swapaxes(0, 1)
+        rest = swap_halves(pair, lon, bit, (me // bit) % 2 == 0)
+        bit *= 2
+    share = rest[0]
+    other = lax.ppermute(share, "ens", [(0, 1), (1, 0)])
+    return jnp.concatenate(
+        [jnp.where(first, share, other), jnp.where(first, other, share)], axis=0
+    )
+
+
 def body(inputs, layer_norm_gain, w_qkv, w_out, w_head, target):
     members, lat, cols, width = inputs.shape
     chans = target.shape[-1]
@@ -284,14 +318,14 @@
     for j in range(CHUNKS):
         g, acc = block_call(arrived[j], gain, w_qkv, w_out, w_head, acc, j == CHUNKS - 1)
         grads.append(lax.all_to_all(g, axes, split_axis=0, concat_axis=0, tiled=True))
+    acc, *grads[:-1] = lax.optimization_barrier((acc, *grads[:-1]))
     grad = jnp.concatenate([g.transpose(1, 0, 2, 3) for g in grads], axis=0)
     grad_input = (
         grad.reshape(each, owners, lat, members, width)
         .transpose(3, 2, 0, 1, 4)
         .reshape(members, lat, cols, width)
     )
-    share = lax.psum_scatter(acc, ("col", "spread"), scatter_dimension=0, tiled=True)
-    share = lax.psum(share, "ens").astype(f32)
+    share = reduce_rows(acc).astype(f32)
     grad_qkv = share[:, : 3 * width]
     grad_out = share[:, 3 * width : 4 * width]
     grad_head = share[:, 4 * width :]

time: 296 us -> 187 us (0.63)
  blocking collectives: 113 us -> 35.7 us
  Pallas kernels: 112 us -> 66.6 us
  waiting for transfers between devices: 22.4 us -> 45.6 us
  between operations: 14.1 us -> 0.81 us
  local copies, waits for them, and re-layouts: 14.1 us -> 9.31 us
  other arithmetic: 2.46 us -> 7.19 us
  starting transfers between devices: 16.7 us -> 21.2 us
    all_to_all x3 -> x0, blocking collectives: 69.9 us -> none  [body(): lax.all_to_all(g, axes, split_axis=0, concat_axis=0, tiled=True)]
    pallas_call x4 -> x2, Pallas kernels: 112 us -> 66.6 us  [block_call(): pl.pallas_call(functools.partial(block_kernel, members, width, chans, pre...]
    ppermute x0 -> x5, waiting for transfers between devices: none -> 45.5 us  [the longest x4 45.5 us: swap_halves(): sent = lax.ppermute(jnp.where(keep_first, pair[1], pair[0]), axes, swap)]
    all_to_all x1 -> x2, waiting for transfers between devices: 9.64 us -> 0.01 us  [body(): lax.all_to_all(g, axes, split_axis=0, concat_axis=0, tiled=True)]
    psum x1 -> x0, waiting for transfers between devices: 7.97 us -> none  [body(): share = lax.psum(share, 'ens').astype(f32)]
    all_to_all x2 -> x1, blocking collectives: 43.5 us -> 35.7 us  [body(): lax.all_to_all(part, axes, split_axis=0, concat_axis=0, tiled=True)]
    ppermute x0 -> x5, starting transfers between devices: none -> 6.52 us  [the longest x4 6.45 us: swap_halves(): sent = lax.ppermute(jnp.where(keep_first, pair[1], pair[0]), axes, swap)]
    all_to_all x2 -> x1, starting transfers between devices: 9.54 us -> 3.83 us  [body(): lax.all_to_all(part, axes, split_axis=0, concat_axis=0, tiled=True)]
  transfers between devices with their start and end apart: 5 -> 8, of which waited for: 3 -> 4; matrix products, arithmetic and copies ran while one was open for 1% -> 2% of each run, Pallas kernels for 28% -> 36%
where the time goes in v2:
time: 187 us; the launch traced here: 186 us
  Pallas kernels  66.6 us (36%)
  waiting for transfers between devices  45.6 us (24%)
  blocking collectives  35.7 us (19%)
  starting transfers between devices  21.2 us (11%)
  local copies, waits for them, and re-layouts  9.31 us (5%)
  other arithmetic  7.19 us (4%)
    pallas_call x2, Pallas kernels, block_call(): pl.pallas_call(functools.partial(block_kernel, members, width, chans, pre...  66.6 us
    ppermute x4, waiting for transfers between devices, swap_halves(): sent = lax.ppermute(jnp.where(keep_first, pair[1], pair[0]), axes, swap)  45.5 us
    all_to_all x1, blocking collectives, body(): lax.all_to_all(part, axes, split_axis=0, concat_axis=0, tiled=True)  35.7 us
    all_to_all x2, starting transfers between devices, body(): lax.all_to_all(g, axes, split_axis=0, concat_axis=0, tiled=True)  10.8 us
    ppermute x4, starting transfers between devices, swap_halves(): sent = lax.ppermute(jnp.where(keep_first, pair[1], pair[0]), axes, swap)  6.45 us
    all_to_all x1, starting transfers between devices, body(): lax.all_to_all(part, axes, split_axis=0, concat_axis=0, tiled=True)  3.83 us
  transfers between devices with their start and end apart: 8, of which 4 were waited for; matrix products, arithmetic and copies ran while one was open for 2% of the time, Pallas kernels for 36%

profile of v2, /device:TPU:0, one launch (start us, length us, event | category | flops | bytes accessed | tf_op | source)
XLA Modules:
  0.0 186.4 jit_solution(11058172333204912160)
XLA Ops:
  0.6 1.0 fusion.10
  1.6 0.1 copy.48
  1.7 2.8 %copy.31 = bf16[4,8,4,16,512]{4,1,0,2,3:T(8,128)(2,1)S(1)} copy(bf16[4,8,4,16,512]{4,3,2,1,0:T(8,128)(2,1)} %bitcast.90) | data formatting | bytes 4194304 | tf_op jit(solution)/shard_map/reshape | solution.py:306
  4.5 1.2 fusion.3
  5.7 35.7 %all_to_all.20.refs_0_ = bf16[16,2,8,2176]{3,2,1,0:T(8,128)(2,1)S(1)} all-to-all(bf16[16,2,8,2176]{3,2,1,0:T(8,128)(2,1)S(1)} %get-tuple-element.16), channel_id=1, replica_groups=mesh['groups'=2,'lon'=8,'ens'=2] {'lon','ens'}, dimensions={0} | all-to-all | bytes 2228224 | tf_op jit(solution)/shard_map/all_to_all | solution.py:315
  41.4 0.0 copy-start.2
  41.4 0.0 copy-start.3
  41.4 0.0 copy-start.4
  41.4 3.8 %all-to-all-start = ((bf16[16,2,8,2176]{3,2,1,0:T(8,128)(2,1)}), bf16[16,2,8,2176]{3,2,1,0:T(8,128)(2,1)S(1)}, u32[]{:S(2)}, u32[]{:S(2)}) async-start(bf16[16,2,8,2176]{3,2,1,0:T(8,128)(2,1)} %get-tuple-element.17), calls=%async_computation | async-start | bytes 2228224 | tf_op jit(solution)/shard_map/all_to_all | solution.py:315
  45.2 0.0 copy-done.2
  45.2 0.0 copy-done.3
  45.2 0.0 copy-done.4
  45.2 0.0 copy-start
  45.3 1.4 copy-done
  46.7 32.5 %grid_block.2 = (bf16[16,2,8,2048]{3,2,1,0:T(8,128)(2,1)}, f32[512,2176]{1,0:T(8,128)}) custom-call(bf16[16,2,8,2176]{3,2,1,0:T(8,128)(2,1)S(1)} %all_to_all.20.refs_0_, f32[1,512]{1,0:T(1,128)S(1)} %bitcast.78, bf16[512,1536]{1,0:T(8,128)(2,1)S(1)} %copy-done, bf16[512,512]{1,0:T(8,128)(2,1)S(1)} %copy-done.2, bf16[512,128]{1,0:T(8,128)(2,1)S(1)} %copy-done.3), custom_call_target="tpu_custom_call" | custom-call | flops 16000000000 | bytes 16000000 | tf_op jit(solution)/shard_map/grid_block/pallas_call | solution.py:231
  79.2 0.0 copy-start.1
  79.2 0.0 all-to-all-done.refs_0_
  79.2 6.2 %all-to-all-start.2 = ((bf16[16,2,8,2048]{3,2,1,0:T(8,128)(2,1)}), bf16[16,2,8,2048]{3,2,1,0:T(8,128)(2,1)}, u32[]{:S(2)}, u32[]{:S(2)}) async-start(bf16[16,2,8,2048]{3,2,1,0:T(8,128)(2,1)} %get-tuple-element.12), calls=%async_computation.2 | async-start | bytes 2097152 | tf_op jit(solution)/shard_map/all_to_all | solution.py:320
  85.4 0.0 copy-done.1
  85.4 34.1 %grid_block.3 = (bf16[16,2,8,2048]{3,2,1,0:T(8,128)(2,1)}, bf16[512,2176]{1,0:T(8,128)(2,1)}) custom-call(bf16[16,2,8,2176]{3,2,1,0:T(8,128)(2,1)S(1)} %all-to-all-done.refs_0_, f32[1,512]{1,0:T(1,128)S(1)} %bitcast.79, bf16[512,1536]{1,0:T(8,128)(2,1)S(1)} %copy-done.1, bf16[512,512]{1,0:T(8,128)(2,1)S(1)} %copy-done.2, bf16[512,128]{1,0:T(8,128)(2,1)S(1)} %copy-done.3, ...), custom_call_target="tpu_custom_call" | custom-call | flops 16000000000 | bytes 16000000 | tf_op jit(solution)/shard_map/grid_block/pallas_call | solution.py:231
  119.5 0.0 all-to-all-done.2
  119.5 1.8 copy.47
  121.3 0.1 select_bitcast_fusion
  121.4 0.4 collective-permute-start
  121.8 2.5 %collective-permute-done = bf16[8,32,2176]{2,1,0:T(8,128)(2,1)} collective-permute-done((bf16[8,32,2176]{2,1,0:T(8,128)(2,1)S(1)}, bf16[8,32,2176]{2,1,0:T(8,128)(2,1)}, u32[]{:S(2)}, u32[]{:S(2)}) %collective-permute-start) | collective-permute-done | bytes 1114144 | tf_op jit(solution)/shard_map/ppermute | solution.py:271
  124.4 1.6 fusion
  126.0 0.1 fusion.5
  126.1 1.9 %collective-permute-start.1 = (bf16[4,32,2176]{2,1,0:T(8,128)(2,1)S(1)}, bf16[4,32,2176]{2,1,0:T(8,128)(2,1)S(1)}, u32[]{:S(2)}, u32[]{:S(2)}) collective-permute-start(bf16[4,32,2176]{2,1,0:T(8,128)(2,1)S(1)} %fusion.5), channel_id=1, source_target_pairs={{0,2},{2,0},{4,6},{6,4},{8,10},{10,8},{12,14},{14,12},{1,3},{3,1},... | collective-permute-start | bytes 1671176 | tf_op jit(solution)/shard_map/ppermute | solution.py:271
  128.0 13.0 %collective-permute-done.1 = bf16[4,32,2176]{2,1,0:T(8,128)(2,1)S(1)} collective-permute-done((bf16[4,32,2176]{2,1,0:T(8,128)(2,1)S(1)}, bf16[4,32,2176]{2,1,0:T(8,128)(2,1)S(1)}, u32[]{:S(2)}, u32[]{:S(2)}) %collective-permute-start.1) | collective-permute-done | bytes 557088 | tf_op jit(solution)/shard_map/ppermute | solution.py:271
  141.0 0.2 fusion.4
  141.3 1.7 collective-permute-start.2
  143.0 4.7 %all-to-all-start.3 = ((bf16[16,2,8,2048]{3,2,1,0:T(8,128)(2,1)}), bf16[16,2,8,2048]{3,2,1,0:T(8,128)(2,1)S(1)}, u32[]{:S(2)}, u32[]{:S(2)}) async-start(bf16[16,2,8,2048]{3,2,1,0:T(8,128)(2,1)} %get-tuple-element.14), calls=%async_computation.3 | async-start | bytes 2097152 | tf_op jit(solution)/shard_map/all_to_all | solution.py:320
  147.7 1.8 collective-permute-done.2
  149.5 0.1 fusion.7
  149.6 2.4 %collective-permute-start.3 = (bf16[1,32,2176]{2,1,0:T(8,128)(2,1)S(1)}, bf16[1,32,2176]{2,1,0:T(8,128)(2,1)S(1)}, u32[]{:S(2)}, u32[]{:S(2)}) collective-permute-start(bf16[1,32,2176]{2,1,0:T(8,128)(2,1)S(1)} %broadcast_select_fusion), channel_id=1, source_target_pairs={{0,8},{2,10},{4,12},{6,14},{8,0},{10,2},{12,4},{14,6},{1,9},{3,11}... | collective-permute-start | bytes 417800 | tf_op jit(solution)/shard_map/ppermute | solution.py:271
  152.0 28.2 %collective-permute-done.3 = bf16[1,32,2176]{2,1,0:T(8,128)(2,1)S(1)} collective-permute-done((bf16[1,32,2176]{2,1,0:T(8,128)(2,1)S(1)}, bf16[1,32,2176]{2,1,0:T(8,128)(2,1)S(1)}, u32[]{:S(2)}, u32[]{:S(2)}) %collective-permute-start.3) | collective-permute-done | bytes 139296 | tf_op jit(solution)/shard_map/ppermute | solution.py:271
  180.2 0.1 fusion.11
  180.2 0.1 collective-permute-start.4
  180.3 0.0 all-to-all-done.3
  180.3 1.4 pad_maximum_fusion
  181.7 2.5 %copy.33 = bf16[4,8,4,16,512]{4,3,2,1,0:T(8,128)(2,1)} copy(bf16[4,8,4,16,512]{4,1,0,2,3:T(8,128)(2,1)S(1)} %bitcast.85) | data formatting | bytes 4194304 | tf_op jit(solution)/shard_map/transpose | solution.py:325
  184.2 0.0 collective-permute-done.4
  184.3 0.7 maximum_convert_fusion.1
  185.0 0.6 maximum_convert_fusion.2
  185.6 0.8 slice.72
  (4 shorter events, 0.1 us)
Async XLA Ops:
  41.4 3.8 %copy-start.2 = (bf16[512,512]{1,0:T(8,128)(2,1)S(1)}, bf16[512,512]{1,0:T(8,128)(2,1)}, u32[]{:S(2)}) copy-start(bf16[512,512]{1,0:T(8,128)(2,1)} %refs_3_.3) | copy-start | bytes 1572868
  41.4 3.9 %copy-start.3 = (bf16[512,128]{1,0:T(8,128)(2,1)S(1)}, bf16[512,128]{1,0:T(8,128)(2,1)}, u32[]{:S(2)}) copy-start(bf16[512,128]{1,0:T(8,128)(2,1)} %refs_4_.3) | copy-start | bytes 393220
  41.4 3.9 %copy-start.4 = (f32[512]{0:T(512)S(1)}, f32[512]{0:T(512)}, u32[]{:S(2)}) copy-start(f32[512]{0:T(512)} %param.7) | copy-start | bytes 6148
  41.4 37.8 %all-to-all-start = ((bf16[16,2,8,2176]{3,2,1,0:T(8,128)(2,1)}), bf16[16,2,8,2176]{3,2,1,0:T(8,128)(2,1)S(1)}, u32[]{:S(2)}, u32[]{:S(2)}) async-start(bf16[16,2,8,2176]{3,2,1,0:T(8,128)(2,1)} %get-tuple-element.17), calls=%async_computation | async-start | bytes 2228224 | tf_op jit(solution)/shard_map/all_to_all | solution.py:315
  45.2 1.4 copy-start
  79.2 6.2 %copy-start.1 = (bf16[512,1536]{1,0:T(8,128)(2,1)S(1)}, bf16[512,1536]{1,0:T(8,128)(2,1)}, u32[]{:S(2)}) copy-start(bf16[512,1536]{1,0:T(8,128)(2,1)} %refs_2_.3) | copy-start | bytes 4718596
  79.2 40.3 %all-to-all-start.2 = ((bf16[16,2,8,2048]{3,2,1,0:T(8,128)(2,1)}), bf16[16,2,8,2048]{3,2,1,0:T(8,128)(2,1)}, u32[]{:S(2)}, u32[]{:S(2)}) async-start(bf16[16,2,8,2048]{3,2,1,0:T(8,128)(2,1)} %get-tuple-element.12), calls=%async_computation.2 | async-start | bytes 2097152 | tf_op jit(solution)/shard_map/all_to_all | solution.py:320
  121.4 3.0 %collective-permute-start = (bf16[8,32,2176]{2,1,0:T(8,128)(2,1)S(1)}, bf16[8,32,2176]{2,1,0:T(8,128)(2,1)}, u32[]{:S(2)}, u32[]{:S(2)}) collective-permute-start(bf16[8,32,2176]{2,1,0:T(8,128)(2,1)S(1)} %select_bitcast_fusion), channel_id=1, source_target_pairs={{0,1},{1,0},{2,3},{3,2},{4,5},{5,4},{6,7},{7,6},{8,9},{9,8},{10,11... | collective-permute-start | bytes 3342344 | tf_op jit(solution)/shard_map/ppermute | solution.py:271
  126.1 14.9 %collective-permute-start.1 = (bf16[4,32,2176]{2,1,0:T(8,128)(2,1)S(1)}, bf16[4,32,2176]{2,1,0:T(8,128)(2,1)S(1)}, u32[]{:S(2)}, u32[]{:S(2)}) collective-permute-start(bf16[4,32,2176]{2,1,0:T(8,128)(2,1)S(1)} %fusion.5), channel_id=1, source_target_pairs={{0,2},{2,0},{4,6},{6,4},{8,10},{10,8},{12,14},{14,12},{1,3},{3,1},... | collective-permute-start | bytes 1671176 | tf_op jit(solution)/shard_map/ppermute | solution.py:271
  141.3 8.2 %collective-permute-start.2 = (bf16[2,32,2176]{2,1,0:T(8,128)(2,1)S(1)}, bf16[2,32,2176]{2,1,0:T(8,128)(2,1)S(1)}, u32[]{:S(2)}, u32[]{:S(2)}) collective-permute-start(bf16[2,32,2176]{2,1,0:T(8,128)(2,1)S(1)} %fusion.8), channel_id=1, source_target_pairs={{0,4},{2,6},{4,0},{6,2},{8,12},{10,14},{12,8},{14,10},{1,5},{3,7},... | collective-permute-start | bytes 835592 | tf_op jit(solution)/shard_map/ppermute | solution.py:271
  143.0 37.3 %all-to-all-start.3 = ((bf16[16,2,8,2048]{3,2,1,0:T(8,128)(2,1)}), bf16[16,2,8,2048]{3,2,1,0:T(8,128)(2,1)S(1)}, u32[]{:S(2)}, u32[]{:S(2)}) async-start(bf16[16,2,8,2048]{3,2,1,0:T(8,128)(2,1)} %get-tuple-element.14), calls=%async_computation.3 | async-start | bytes 2097152 | tf_op jit(solution)/shard_map/all_to_all | solution.py:320
  149.6 30.6 %collective-permute-start.3 = (bf16[1,32,2176]{2,1,0:T(8,128)(2,1)S(1)}, bf16[1,32,2176]{2,1,0:T(8,128)(2,1)S(1)}, u32[]{:S(2)}, u32[]{:S(2)}) collective-permute-start(bf16[1,32,2176]{2,1,0:T(8,128)(2,1)S(1)} %broadcast_select_fusion), channel_id=1, source_target_pairs={{0,8},{2,10},{4,12},{6,14},{8,0},{10,2},{12,4},{14,6},{1,9},{3,11}... | collective-permute-start | bytes 417800 | tf_op jit(solution)/shard_map/ppermute | solution.py:271
  180.2 4.0 %collective-permute-start.4 = (bf16[32,2176]{1,0:T(8,128)(2,1)S(1)}, bf16[32,2176]{1,0:T(8,128)(2,1)S(1)}, u32[]{:S(2)}, u32[]{:S(2)}) collective-permute-start(bf16[32,2176]{1,0:T(8,128)(2,1)S(1)} %fusion.11), channel_id=1, source_target_pairs={{0,1},{1,0},{2,3},{3,2},{4,5},{5,4},{6,7},{7,6},{8,9},{9,8},{10,11... | collective-permute-start | bytes 417800 | tf_op jit(solution)/shard_map/ppermute | solution.py:291

commit v3 on v2

--- a/solution.py
+++ b/solution.py
@@ -14,7 +14,8 @@
 smooth_width = 0.25
 loss_scale = 32.0
 LOG2E = 1.4426950408889634
-CHUNKS = 2
+TIE_EARLY = 1
+TIE_LATE = 4
 
 bf16 = jnp.bfloat16
 f32 = jnp.float32
@@ -48,15 +49,27 @@
     return out
 
 
-def block_kernel(members, width, chans, first, *refs):
-    if first:
-        x_ref, gain_ref, wqkv_ref, wout_ref, whead_ref, gx_ref, acc_ref = refs[:7]
-        scratch = refs[7:]
-        prev_ref = None
+def block_kernel(members, width, chans, first, last, *refs):
+    x_ref, gain_ref, wqkv_hbm, wout_hbm, whead_hbm = refs[:5]
+    refs = refs[5:]
+    if not first:
+        prev_ref, refs = refs[0], refs[1:]
+    gx_ref, refs = refs[0], refs[1:]
+    if last:
+        mine_ref, sent_ref, refs = refs[0], refs[1], refs[2:]
     else:
-        x_ref, gain_ref, wqkv_ref, wout_ref, whead_ref, prev_ref, gx_ref, acc_ref = refs[:8]
-        scratch = refs[8:]
-    xf, normed, normed_t, qkv, g_qkv, att, probs, bout, g_pred, g_block, g_att, mask_ref, acc = scratch
+        acc_ref, refs = refs[0], refs[1:]
+    xf, normed, normed_t, qkv, g_qkv, att, probs, bout, g_pred, g_block, g_att, mask_ref, acc = (
+        refs[:13]
+    )
+    wqkv_ref, wout_ref, whead_ref, sems = refs[13:]
+    fetches = [
+        pltpu.make_async_copy(wqkv_hbm, wqkv_ref, sems.at[0]),
+        pltpu.make_async_copy(wout_hbm, wout_ref, sems.at[1]),
+        pltpu.make_async_copy(whead_hbm, whead_ref, sems.at[2]),
+    ]
+    if not first:
+        fetches.append(pltpu.make_async_copy(prev_ref, acc, sems.at[3]))
     cells = CELLS * CELLS
     rows = members * cells
     half = members // 2
@@ -69,10 +82,10 @@
 
     @pl.when(step == 0)
     def _():
+        for fetch in fetches:
+            fetch.start()
         if first:
             acc[...] = jnp.zeros_like(acc)
-        else:
-            acc[...] = prev_ref[...]
         row_head = lax.broadcasted_iota(jnp.int32, (4 * cells, pack), 0) // cells
         lane_head = lax.broadcasted_iota(jnp.int32, (4 * cells, pack), 1) // dim
         mask_ref[...] = jnp.where(row_head == lane_head, 1.0, 0.0).astype(bf16)
@@ -96,6 +109,10 @@
         centered = x - jnp.mean(x, axis=-1, keepdims=True)
         var = jnp.mean(centered * centered, axis=-1, keepdims=True)
         normed[at, :] = (centered * lax.rsqrt(var + eps_norm) * gain).astype(bf16)
+
+    @pl.when(step == 0)
+    def _():
+        fetches[0].wait()
 
     @pl.loop(0, 3 * width // tile)
     def _(n):
@@ -118,6 +135,11 @@
         outs = [dot_rows(weights[p].astype(bf16), part(p, 2)) for p in each]
         for p in each:
             att[at, p * pack : (p + 1) * pack] = diagonal(outs[p], lane, dim).astype(bf16)
+
+    @pl.when(step == 0)
+    def _():
+        for fetch in fetches[1:]:
+            fetch.wait()
 
     bout[...] = (xf[...] + dot(att[...], wout_ref[...])).astype(bf16)
     pred = dot(bout[...], whead_ref[...]).astype(bf16).astype(f32).reshape(members, cells, chans)
@@ -179,6 +201,19 @@
 
     acc[:, 4 * width :] += dot_rows(bout[...], g_pred[...])
 
+    @pl.when(step == pl.num_programs(0) - 1)
+    def _():
+        if last:
+            core = lax.axis_index("ens")
+            shards, piece, _ = mine_ref.shape
+            for b in range(shards):
+                low = acc[2 * b * piece : (2 * b + 1) * piece, :]
+                high = acc[(2 * b + 1) * piece : (2 * b + 2) * piece, :]
+                mine_ref[b] = jnp.where(core == 0, low, high).astype(bf16)
+                sent_ref[b] = jnp.where(core == 0, high, low).astype(bf16)
+        else:
+            pltpu.make_async_copy(acc, acc_ref, sems.at[3]).start()
+
     @pl.loop(0, width // tile)
     def _(n):
         at = pl.ds(pl.multiple_of(n * tile, tile), tile)
@@ -203,43 +238,50 @@
                 c * CELLS : (c + 1) * CELLS, :
             ].astype(bf16)
 
-    @pl.when(step == pl.num_programs(0) - 1)
-    def _():
-        acc_ref[...] = acc[...].astype(acc_ref.dtype)
-
-
-def block_call(x, gain, w_qkv, w_out, w_head, prev, last):
-    sources, count, lat, lanes = x.shape
+    if not last:
+
+        @pl.when(step == pl.num_programs(0) - 1)
+        def _():
+            pltpu.make_async_copy(acc, acc_ref, sems.at[3]).wait()
+
+
+def block_call(x, gain, w_qkv, w_out, w_head, prev, shards):
+    sources, count, lat = x.shape[:3]
     width, chans = w_head.shape
-    members = 2 * ((lanes - chans) // width)
+    members = 8
+    lanes = members // 2 * width
     rows = members * CELLS * CELLS
     total = 4 * width + chans
     whole = lambda shape: pl.BlockSpec(shape, lambda i: (0,) * len(shape))
+    anywhere = pl.BlockSpec(memory_space=pl.ANY)
     in_specs = [
-        pl.BlockSpec((sources, 1, lat, lanes), lambda i: (0, i, 0, 0)),
+        pl.BlockSpec((sources, 1, lat, lanes + chans), lambda i: (0, i, 0, 0)),
         whole((1, width)),
-        whole(w_qkv.shape),
-        whole(w_out.shape),
-        whole(w_head.shape),
+        anywhere,
+        anywhere,
+        anywhere,
     ]
     args = [x, gain, w_qkv, w_out, w_head]
     if prev is not None:
-        in_specs.append(whole((width, total)))
+        in_specs.append(anywhere)
         args.append(prev)
     cells = CELLS * CELLS
     pack = 4 * (width // HEADS)
+    out_specs = [pl.BlockSpec((sources, 1, lat, lanes), lambda i: (0, i, 0, 0))]
+    out_shape = [jax.ShapeDtypeStruct((sources, count, lat, lanes), bf16)]
+    if shards:
+        sums = (shards, width // shards // 2, total)
+        out_specs += [whole(sums)] * 2
+        out_shape += [jax.ShapeDtypeStruct(sums, bf16)] * 2
+    else:
+        out_specs.append(anywhere)
+        out_shape.append(jax.ShapeDtypeStruct((width, total), f32))
     return pl.pallas_call(
-        functools.partial(block_kernel, members, width, chans, prev is None),
+        functools.partial(block_kernel, members, width, chans, prev is None, shards > 0),
         grid=(count,),
         in_specs=in_specs,
-        out_specs=[
-            pl.BlockSpec((sources, 1, lat, lanes - chans), lambda i: (0, i, 0, 0)),
-            whole((width, total)),
-        ],
-        out_shape=[
-            jax.ShapeDtypeStruct((sources, count, lat, lanes - chans), bf16),
-            jax.ShapeDtypeStruct((width, total), bf16 if last else f32),
-        ],
+        out_specs=out_specs,
+        out_shape=out_shape,
         scratch_shapes=[
             pltpu.VMEM((rows, width), f32),
             pltpu.VMEM((rows, width), bf16),
@@ -254,6 +296,10 @@
             pltpu.VMEM((rows, width), bf16),
             pltpu.VMEM((4 * cells, pack), bf16),
             pltpu.VMEM((width, total), f32),
+            pltpu.VMEM(w_qkv.shape, bf16),
+            pltpu.VMEM(w_out.shape, bf16),
+            pltpu.VMEM(w_head.shape, bf16),
+            pltpu.SemaphoreType.DMA((4,)),
         ],
         compiler_params=pltpu.CompilerParams(vmem_limit_bytes=48 * 1024 * 1024),
         cost_estimate=pl.CostEstimate(
@@ -264,34 +310,43 @@
 
 
 def swap_halves(pair, axes, bit, keep_first):
+    kept = jnp.where(keep_first, pair[0], pair[1])
+    return swap_sum(kept, jnp.where(keep_first, pair[1], pair[0]), axes, bit)
+
+
+def swap_sum(kept, given, axes, bit):
     count = 1
     for axis in axes:
         count *= lax.axis_size(axis)
     swap = [(i, i ^ bit) for i in range(count)]
-    sent = lax.ppermute(jnp.where(keep_first, pair[1], pair[0]), axes, swap)
-    kept = jnp.where(keep_first, pair[0], pair[1])
-    return (kept.astype(f32) + sent.astype(f32)).astype(pair.dtype)
-
-
-def reduce_rows(grad):
+    taken = lax.ppermute(given, axes, swap)
+    return (kept.astype(f32) + taken.astype(f32)).astype(kept.dtype)
+
+
+def reduce_rows(mine, given, early, late):
     lon = ("col", "spread")
     shards = lax.axis_size("col") * lax.axis_size("spread")
     me = lax.axis_index(lon)
     first = lax.axis_index("ens") == 0
-    block = grad.shape[0] // shards
-    rest = grad.reshape(shards, 2, block // 2, -1).transpose(1, 0, 2, 3)
-    rest = swap_halves(rest, ("ens",), 1, first)
+    rest = swap_sum(mine, given, ("ens",), 1)
     bit = 1
     while bit < shards:
         left = rest.shape[0]
         pair = rest.reshape(left // 2, 2, *rest.shape[1:]).swapaxes(0, 1)
+        if bit == TIE_EARLY:
+            pair, early = lax.optimization_barrier((pair, early))
+        if bit == TIE_LATE:
+            pair, late = lax.optimization_barrier((pair, late))
         rest = swap_halves(pair, lon, bit, (me // bit) % 2 == 0)
         bit *= 2
     share = rest[0]
+    if TIE_LATE is None:
+        share, late = lax.optimization_barrier((share, late))
     other = lax.ppermute(share, "ens", [(0, 1), (1, 0)])
-    return jnp.concatenate(
+    share = jnp.concatenate(
         [jnp.where(first, share, other), jnp.where(first, other, share)], axis=0
     )
+    return share, early, late
 
 
 def body(inputs, layer_norm_gain, w_qkv, w_out, w_head, target):
@@ -300,32 +355,45 @@
     axes = ("col", "ens")
     owners = lax.axis_size("col") * lax.axis_size("ens")
     each = cols // owners
+    shards = lax.axis_size("col") * lax.axis_size("spread")
     gain = layer_norm_gain.reshape(1, width)
+    lanes = members * width
+    move = lambda g: lax.all_to_all(g, axes, split_axis=0, concat_axis=0, tiled=True)
     high = lax.reduce_precision(target, 8, 7)
     target_part = jnp.where(lax.axis_index("ens") == 0, high, target - high).astype(bf16)
-    send_x = inputs.reshape(members, lat, each, owners, width).transpose(2, 3, 1, 0, 4)
-    send_x = send_x.reshape(each, owners, lat, members * width)
-    send_t = target_part.reshape(lat, each, owners, chans).transpose(1, 2, 0, 3)
-    send = jnp.concatenate([send_x, send_t], axis=-1)
-
-    per = each // CHUNKS
-    arrived = []
-    for j in range(CHUNKS):
-        part = send[j * per : (j + 1) * per].transpose(1, 0, 2, 3)
-        arrived.append(lax.all_to_all(part, axes, split_axis=0, concat_axis=0, tiled=True))
-    acc = None
-    grads = []
-    for j in range(CHUNKS):
-        g, acc = block_call(arrived[j], gain, w_qkv, w_out, w_head, acc, j == CHUNKS - 1)
-        grads.append(lax.all_to_all(g, axes, split_axis=0, concat_axis=0, tiled=True))
-    acc, *grads[:-1] = lax.optimization_barrier((acc, *grads[:-1]))
-    grad = jnp.concatenate([g.transpose(1, 0, 2, 3) for g in grads], axis=0)
-    grad_input = (
-        grad.reshape(each, owners, lat, members, width)
-        .transpose(3, 2, 0, 1, 4)
-        .reshape(members, lat, cols, width)
-    )
-    share = reduce_rows(acc).astype(f32)
+
+    def outgoing(start, count):
+        span = slice(start * owners, (start + count) * owners)
+        send_x = inputs[:, :, span].reshape(members, lat, count, owners, width)
+        send_x = send_x.transpose(3, 2, 1, 0, 4).reshape(owners, count, lat, lanes)
+        send_t = target_part[:, span].reshape(lat, count, owners, chans).transpose(2, 1, 0, 3)
+        return jnp.concatenate([send_x, send_t], axis=-1)
+
+    lead, main = each // 4, each // 2
+    tail = each - lead - main
+    x_lead = move(outgoing(0, lead))
+    x_main = move(outgoing(lead, main))
+    weights = (gain, w_qkv, w_out, w_head)
+    g_lead, acc = block_call(x_lead, *weights, None, 0)
+    both = move(jnp.concatenate([outgoing(lead + main, tail), g_lead], axis=-1))
+    g_main, acc = block_call(x_main, *weights, acc, 0)
+    g_main = move(g_main)
+    g_tail, mine, given = block_call(both, *weights, acc, shards)
+    g_tail = move(g_tail)
+    back_lead = both[..., lanes + chans :]
+    share, (g_main,), g_tail = reduce_rows(mine, given, [g_main], g_tail)
+    share = share.astype(f32)
+    columns = (
+        lambda g: g.reshape(owners, -1, lat, members, width)
+        .transpose(3, 2, 1, 0, 4)
+        .reshape(members, lat, -1, width)
+    )
+    ready = jnp.concatenate([columns(back_lead), columns(g_main)], axis=2)
+    ready = jnp.pad(ready, ((0, 0), (0, 0), (0, tail * owners), (0, 0)))
+    ready = lax.optimization_barrier(ready)
+    grad_input = lax.dynamic_update_slice(
+        ready, columns(g_tail), (0, 0, (lead + main) * owners, 0)
+    )
     grad_qkv = share[:, : 3 * width]
     grad_out = share[:, 3 * width : 4 * width]
     grad_head = share[:, 4 * width :]

time: 187 us -> 168 us (0.90)
  blocking collectives: 35.7 us -> 0 us
  starting transfers between devices: 21.2 us -> 36.8 us
  local copies, waits for them, and re-layouts: 9.31 us -> 11.9 us
    all_to_all x1 -> x0, blocking collectives: 35.7 us -> none  [body(): lax.all_to_all(part, axes, split_axis=0, concat_axis=0, tiled=True)]
    ppermute x4, waiting for transfers between devices: 45.5 us -> 25.4 us  [swap_sum(): taken = lax.ppermute(given, axes, swap)]
    all_to_all x2 -> x5, starting transfers between devices: 10.8 us -> 30 us  [body(): lax.all_to_all(g, axes, split_axis=0, concat_axis=0, tiled=True)]
    all_to_all x2 -> x5, waiting for transfers between devices: 0.01 us -> 17.7 us  [body(): lax.all_to_all(g, axes, split_axis=0, concat_axis=0, tiled=True)]
    unnamed x10 -> x18, local copies, waits for them, and re-layouts: 1.42 us -> 5.27 us
    all_to_all x1 -> x0, starting transfers between devices: 3.83 us -> none  [body(): lax.all_to_all(part, axes, split_axis=0, concat_axis=0, tiled=True)]
    reshape x3 -> x4, local copies, waits for them, and re-layouts: 4.64 us -> 0.97 us  [the longest x1 0.58 us: outgoing(): send_x = inputs[:, :, span].reshape(members, lat, count, owners, width)]
    pallas_call x2 -> x3, Pallas kernels: 66.6 us -> 64.8 us  [block_call(): pl.pallas_call(functools.partial(block_kernel, members, width, chans, pre...]
  transfers between devices with their start and end apart: 8 -> 10, of which waited for: 4 -> 7; matrix products, arithmetic and copies ran while one was open for 2% -> 5% of each run, Pallas kernels for 36% -> 39%
where the time goes in v3:
time: 168 us; the launch traced here: 167 us
  Pallas kernels  64.8 us (39%)
  waiting for transfers between devices  44.2 us (26%)
  starting transfers between devices  36.8 us (22%)
  local copies, waits for them, and re-layouts  11.9 us (7%)
  other arithmetic  8.74 us (5%)
    pallas_call x3, Pallas kernels, block_call(): pl.pallas_call(functools.partial(block_kernel, members, width, chans, pre...  64.8 us
    all_to_all x5, starting transfers between devices, body(): lax.all_to_all(g, axes, split_axis=0, concat_axis=0, tiled=True)  30 us
    ppermute x4, waiting for transfers between devices, swap_sum(): taken = lax.ppermute(given, axes, swap)  25.4 us
    all_to_all x5, waiting for transfers between devices, body(): lax.all_to_all(g, axes, split_axis=0, concat_axis=0, tiled=True)  17.7 us
    ppermute x4, starting transfers between devices, swap_sum(): taken = lax.ppermute(given, axes, swap)  6.71 us
    unnamed x18, local copies, waits for them, and re-layouts  5.27 us
  transfers between devices with their start and end apart: 10, of which 7 were waited for; matrix products, arithmetic and copies ran while one was open for 5% of the time, Pallas kernels for 39%

profile of v3, /device:TPU:0, one launch (start us, length us, event | category | flops | bytes accessed | tf_op | source)
XLA Modules:
  0.0 167.4 jit_solution(14910024195242657350)
XLA Ops:
  0.6 1.1 fusion.9
  1.8 0.0 copy-start.8
  1.8 1.3 slice_bitcast_fusion.1
  3.1 0.3 copy.27
  3.4 0.0 slice-start
  3.4 0.8 pad_maximum_fusion.2
  4.3 7.4 %all-to-all-start = ((bf16[16,1,8,2176]{3,2,1,0:T(8,128)(2,1)}), bf16[16,1,8,2176]{3,2,1,0:T(8,128)(2,1)S(1)}, u32[]{:S(2)}, u32[]{:S(2)}) async-start(bf16[16,1,8,2176]{3,2,1,0:T(8,128)(2,1)} %pad_maximum_fusion.2), calls=%async_computation | async-start | bytes 1114112 | tf_op jit(solution)/shard_map/all_to_all | solution.py:361
  11.7 0.0 copy-done.8
  11.7 0.0 slice-start.1
  11.7 0.8 slice-done.1
  12.5 0.0 slice-done
  12.5 0.6 copy.30
  13.1 1.1 pad_maximum_fusion
  14.2 0.0 copy-start.3
  14.2 0.0 copy-start.5
  14.2 12.5 %all-to-all-done.refs_0_ = bf16[16,1,8,2176]{3,2,1,0:T(8,128)(2,1)S(1)} async-done(((bf16[16,1,8,2176]{3,2,1,0:T(8,128)(2,1)}), bf16[16,1,8,2176]{3,2,1,0:T(8,128)(2,1)S(1)}, u32[]{:S(2)}, u32[]{:S(2)}) %all-to-all-start) | async-done | bytes 557088 | tf_op jit(solution)/shard_map/all_to_all | solution.py:361
  26.7 4.2 %all-to-all-start.2 = ((bf16[16,2,8,2176]{3,2,1,0:T(8,128)(2,1)}), bf16[16,2,8,2176]{3,2,1,0:T(8,128)(2,1)S(1)}, u32[]{:S(2)}, u32[]{:S(2)}) async-start(bf16[16,2,8,2176]{3,2,1,0:T(8,128)(2,1)} %pad_maximum_fusion), calls=%async_computation.2 | async-start | bytes 2228224 | tf_op jit(solution)/shard_map/all_to_all | solution.py:361
  30.9 0.3 copy.24
  31.2 0.0 copy-done.3
  31.2 0.0 copy-done.5
  31.3 0.0 copy-done.6
  31.3 0.0 copy-start
  31.3 1.4 copy-done
  32.7 16.0 %grid_block.3 = (bf16[16,1,8,2048]{3,2,1,0:T(8,128)(2,1)S(1)}, f32[512,2176]{1,0:T(8,128)}) custom-call(bf16[16,1,8,2176]{3,2,1,0:T(8,128)(2,1)S(1)} %all-to-all-done.refs_0_, f32[1,512]{1,0:T(1,128)S(1)} %bitcast.96, bf16[512,1536]{1,0:T(8,128)(2,1)S(1)} %copy-done, bf16[512,512]{1,0:T(8,128)(2,1)S(1)} %copy-done.3, bf16[512,128]{1,0:T(8,128)(2,1)S(1)} %copy-done.5), custom_call_target="tpu_custom_call" | custom-call | flops 8000000000 | bytes 16000000 | tf_op jit(solution)/shard_map/grid_block/pallas_call | solution.py:279
  48.7 1.0 pad_maximum_fusion.1
  49.7 5.2 %all-to-all-done.2.refs_0_ = bf16[16,2,8,2176]{3,2,1,0:T(8,128)(2,1)S(1)} async-done(((bf16[16,2,8,2176]{3,2,1,0:T(8,128)(2,1)}), bf16[16,2,8,2176]{3,2,1,0:T(8,128)(2,1)S(1)}, u32[]{:S(2)}, u32[]{:S(2)}) %all-to-all-start.2) | async-done | bytes 1114144 | tf_op jit(solution)/shard_map/all_to_all | solution.py:361
  55.0 7.2 %all-to-all-start.1 = ((bf16[16,1,8,4224]{3,2,1,0:T(8,128)(2,1)}), bf16[16,1,8,4224]{3,2,1,0:T(8,128)(2,1)S(1)}, u32[]{:S(2)}, u32[]{:S(2)}) async-start(bf16[16,1,8,4224]{3,2,1,0:T(8,128)(2,1)} %pad_maximum_fusion.1), calls=%async_computation.1 | async-start | bytes 2162688 | tf_op jit(solution)/shard_map/all_to_all | solution.py:361
  62.2 0.0 copy-start.1
  62.2 1.4 copy-done.1
  63.6 31.9 %grid_block.4 = (bf16[16,2,8,2048]{3,2,1,0:T(8,128)(2,1)}, f32[512,2176]{1,0:T(8,128)}) custom-call(bf16[16,2,8,2176]{3,2,1,0:T(8,128)(2,1)S(1)} %all-to-all-done.2.refs_0_, f32[1,512]{1,0:T(1,128)S(1)} %bitcast.97, bf16[512,1536]{1,0:T(8,128)(2,1)S(1)} %copy-done.1, bf16[512,512]{1,0:T(8,128)(2,1)S(1)} %copy-done.3, bf16[512,128]{1,0:T(8,128)(2,1)S(1)} %copy-done.5, ...), custom_call_target="tpu_custom_call" | custom-call | flops 16000000000 | bytes 16000000 | tf_op jit(solution)/shard_map/grid_block/pallas_call | solution.py:279
  95.5 0.0 all-to-all-done.1.refs_0_
  95.5 6.1 %all-to-all-start.3 = ((bf16[16,2,8,2048]{3,2,1,0:T(8,128)(2,1)}), bf16[16,2,8,2048]{3,2,1,0:T(8,128)(2,1)}, u32[]{:S(2)}, u32[]{:S(2)}) async-start(bf16[16,2,8,2048]{3,2,1,0:T(8,128)(2,1)} %get-tuple-element.20), calls=%async_computation.3 | async-start | bytes 2097152 | tf_op jit(solution)/shard_map/all_to_all | solution.py:361
  101.6 0.0 copy-start.2
  101.6 1.4 copy-done.2
  103.0 1.0 copy-done.4
  104.1 16.8 %grid_block.5 = (bf16[16,1,8,2048]{3,2,1,0:T(8,128)(2,1)}, bf16[8,32,2176]{2,1,0:T(8,128)(2,1)S(1)}, bf16[8,32,2176]{2,1,0:T(8,128)(2,1)S(1)}) custom-call(bf16[16,1,8,4224]{3,2,1,0:T(8,128)(2,1)S(1)} %all-to-all-done.1.refs_0_, f32[1,512]{1,0:T(1,128)S(1)} %bitcast.98, bf16[512,1536]{1,0:T(8,128)(2,1)S(1)} %copy-done.2, bf16[512,512]{1,0:T(8,128)(2,1)S(1)} %copy-done.4, ...), custom_call_target="tpu_custom_call" | custom-call | flops 8000000000 | bytes 16000000 | tf_op jit(solution)/shard_map/grid_block/pallas_call | solution.py:279
  120.9 0.4 collective-permute-start
  121.3 2.5 %collective-permute-done = bf16[8,32,2176]{2,1,0:T(8,128)(2,1)} collective-permute-done((bf16[8,32,2176]{2,1,0:T(8,128)(2,1)S(1)}, bf16[8,32,2176]{2,1,0:T(8,128)(2,1)}, u32[]{:S(2)}, u32[]{:S(2)}) %collective-permute-start) | collective-permute-done | bytes 1114144 | tf_op jit(solution)/shard_map/ppermute | solution.py:322
  123.9 1.5 add_convert_fusion
  125.4 0.1 copy.49
  125.5 0.0 all-to-all-done.3
  125.5 0.1 select_bitcast_fusion
  125.6 1.9 %collective-permute-start.1 = (bf16[4,32,2176]{2,1,0:T(8,128)(2,1)S(1)}, bf16[4,32,2176]{2,1,0:T(8,128)(2,1)}, u32[]{:S(2)}, u32[]{:S(2)}) collective-permute-start(bf16[4,32,2176]{2,1,0:T(8,128)(2,1)S(1)} %select_bitcast_fusion), channel_id=1, source_target_pairs={{0,2},{2,0},{4,6},{6,4},{8,10},{10,8},{12,14},{14,12},{1,3},{3,1},... | collective-permute-start | bytes 1671176 | tf_op jit(solution)/shard_map/ppermute | solution.py:322
  127.5 5.1 %all-to-all-start.4 = ((bf16[16,1,8,2048]{3,2,1,0:T(8,128)(2,1)}), bf16[16,1,8,2048]{3,2,1,0:T(8,128)(2,1)S(1)}, u32[]{:S(2)}, u32[]{:S(2)}) async-start(bf16[16,1,8,2048]{3,2,1,0:T(8,128)(2,1)} %get-tuple-element.23), calls=%async_computation.4 | async-start | bytes 1048576 | tf_op jit(solution)/shard_map/all_to_all | solution.py:361
  132.6 11.4 %collective-permute-done.1 = bf16[4,32,2176]{2,1,0:T(8,128)(2,1)} collective-permute-done((bf16[4,32,2176]{2,1,0:T(8,128)(2,1)S(1)}, bf16[4,32,2176]{2,1,0:T(8,128)(2,1)}, u32[]{:S(2)}, u32[]{:S(2)}) %collective-permute-start.1) | collective-permute-done | bytes 557088 | tf_op jit(solution)/shard_map/ppermute | solution.py:322
  144.1 1.3 fusion.3
  145.4 3.1 %collective-permute-start.2 = (bf16[2,32,2176]{2,1,0:T(8,128)(2,1)S(1)}, bf16[2,32,2176]{2,1,0:T(8,128)(2,1)S(1)}, u32[]{:S(2)}, u32[]{:S(2)}) collective-permute-start(bf16[2,32,2176]{2,1,0:T(8,128)(2,1)S(1)} %fusion.5), channel_id=1, source_target_pairs={{0,4},{2,6},{4,0},{6,2},{8,12},{10,14},{12,8},{14,10},{1,5},{3,7},... | collective-permute-start | bytes 835592 | tf_op jit(solution)/shard_map/ppermute | solution.py:322
  148.5 0.3 copy.50
  148.8 1.8 %copy.33 = bf16[4,8,2,16,512]{4,3,2,1,0:T(8,128)(2,1)S(1)} copy(bf16[4,8,2,16,512]{4,1,0,2,3:T(8,128)(2,1)} %bitcast.23) | data formatting | bytes 2097152 | tf_op jit(solution)/shard_map/transpose | solution.py:388
  150.6 4.4 %collective-permute-done.2 = bf16[2,32,2176]{2,1,0:T(8,128)(2,1)S(1)} collective-permute-done((bf16[2,32,2176]{2,1,0:T(8,128)(2,1)S(1)}, bf16[2,32,2176]{2,1,0:T(8,128)(2,1)S(1)}, u32[]{:S(2)}, u32[]{:S(2)}) %collective-permute-start.2) | collective-permute-done | bytes 278560 | tf_op jit(solution)/shard_map/ppermute | solution.py:322
  155.0 0.1 fusion.6
  155.1 0.0 all-to-all-done.4
  155.1 1.3 collective-permute-start.3
  156.4 0.2 fusion.2
  156.7 7.1 %collective-permute-done.3 = bf16[1,32,2176]{2,1,0:T(8,128)(2,1)S(1)} collective-permute-done((bf16[1,32,2176]{2,1,0:T(8,128)(2,1)S(1)}, bf16[1,32,2176]{2,1,0:T(8,128)(2,1)S(1)}, u32[]{:S(2)}, u32[]{:S(2)}) %collective-permute-start.3) | collective-permute-done | bytes 139296 | tf_op jit(solution)/shard_map/ppermute | solution.py:322
  163.8 0.1 fusion.10
  163.8 0.1 collective-permute-start.4
  163.9 0.3 bitcast_dynamic-update-slice_fusion
  164.2 0.0 copy-start.7
  164.2 1.0 collective-permute-done.4
  165.3 0.7 maximum_convert_fusion.1
  166.0 0.6 maximum_convert_fusion.2
  166.6 0.8 slice.77
  167.4 0.0 copy-done.7
  (9 shorter events, 0.2 us)
Async XLA Ops:
  1.8 9.9 %copy-start.8 = (bf16[8,64,128]{2,0,1:T(8,128)(2,1)}, bf16[8,64,128]{2,0,1:T(8,128)(2,1)S(1)}, u32[]{:S(2)}) copy-start(bf16[8,64,128]{2,0,1:T(8,128)(2,1)S(1)} %fusion.9) | copy-start | bytes 393220
  3.4 9.1 %slice-start = ((bf16[4,8,64,512]{3,2,1,0:T(8,128)(2,1)}), bf16[4,8,32,512]{3,2,1,0:T(8,128)(2,1)S(1)}, s32[]{:S(2)}) async-start(bf16[4,8,64,512]{3,2,1,0:T(8,128)(2,1)} %param.6), calls=%async_computation.5 | async-start | bytes 2097152 | tf_op jit(solution)/shard_map/slice | solution.py:367
  4.3 22.4 %all-to-all-start = ((bf16[16,1,8,2176]{3,2,1,0:T(8,128)(2,1)}), bf16[16,1,8,2176]{3,2,1,0:T(8,128)(2,1)S(1)}, u32[]{:S(2)}, u32[]{:S(2)}) async-start(bf16[16,1,8,2176]{3,2,1,0:T(8,128)(2,1)} %pad_maximum_fusion.2), calls=%async_computation | async-start | bytes 1114112 | tf_op jit(solution)/shard_map/all_to_all | solution.py:361
  11.7 0.8 slice-start.1
  14.2 17.0 %copy-start.3 = (bf16[512,512]{1,0:T(8,128)(2,1)S(1)}, bf16[512,512]{1,0:T(8,128)(2,1)}, u32[]{:S(2)}) copy-start(bf16[512,512]{1,0:T(8,128)(2,1)} %refs_3_.5) | copy-start | bytes 1572868
  14.2 17.0 %copy-start.5 = (bf16[512,128]{1,0:T(8,128)(2,1)S(1)}, bf16[512,128]{1,0:T(8,128)(2,1)}, u32[]{:S(2)}) copy-start(bf16[512,128]{1,0:T(8,128)(2,1)} %refs_4_.5) | copy-start | bytes 393220
  14.2 17.0 %copy-start.6 = (f32[512]{0:T(512)S(1)}, f32[512]{0:T(512)}, u32[]{:S(2)}) copy-start(f32[512]{0:T(512)} %param.7) | copy-start | bytes 6148
  26.7 28.3 %all-to-all-start.2 = ((bf16[16,2,8,2176]{3,2,1,0:T(8,128)(2,1)}), bf16[16,2,8,2176]{3,2,1,0:T(8,128)(2,1)S(1)}, u32[]{:S(2)}, u32[]{:S(2)}) async-start(bf16[16,2,8,2176]{3,2,1,0:T(8,128)(2,1)} %pad_maximum_fusion), calls=%async_computation.2 | async-start | bytes 2228224 | tf_op jit(solution)/shard_map/all_to_all | solution.py:361
  31.3 1.4 copy-start
  55.0 40.6 %all-to-all-start.1 = ((bf16[16,1,8,4224]{3,2,1,0:T(8,128)(2,1)}), bf16[16,1,8,4224]{3,2,1,0:T(8,128)(2,1)S(1)}, u32[]{:S(2)}, u32[]{:S(2)}) async-start(bf16[16,1,8,4224]{3,2,1,0:T(8,128)(2,1)} %pad_maximum_fusion.1), calls=%async_computation.1 | async-start | bytes 2162688 | tf_op jit(solution)/shard_map/all_to_all | solution.py:361
  62.2 1.4 copy-start.1
  95.5 30.0 %all-to-all-start.3 = ((bf16[16,2,8,2048]{3,2,1,0:T(8,128)(2,1)}), bf16[16,2,8,2048]{3,2,1,0:T(8,128)(2,1)}, u32[]{:S(2)}, u32[]{:S(2)}) async-start(bf16[16,2,8,2048]{3,2,1,0:T(8,128)(2,1)} %get-tuple-element.20), calls=%async_computation.3 | async-start | bytes 2097152 | tf_op jit(solution)/shard_map/all_to_all | solution.py:361
  101.6 1.4 copy-start.2
  103.0 1.0 copy-start.4
  120.9 3.0 %collective-permute-start = (bf16[8,32,2176]{2,1,0:T(8,128)(2,1)S(1)}, bf16[8,32,2176]{2,1,0:T(8,128)(2,1)}, u32[]{:S(2)}, u32[]{:S(2)}) collective-permute-start(bf16[8,32,2176]{2,1,0:T(8,128)(2,1)S(1)} %get-tuple-element.19), channel_id=1, source_target_pairs={{0,1},{1,0},{2,3},{3,2},{4,5},{5,4},{6,7},{7,6},{8,9},{9,8},{10,11... | collective-permute-start | bytes 3342344 | tf_op jit(solution)/shard_map/ppermute | solution.py:322
  125.6 18.5 %collective-permute-start.1 = (bf16[4,32,2176]{2,1,0:T(8,128)(2,1)S(1)}, bf16[4,32,2176]{2,1,0:T(8,128)(2,1)}, u32[]{:S(2)}, u32[]{:S(2)}) collective-permute-start(bf16[4,32,2176]{2,1,0:T(8,128)(2,1)S(1)} %select_bitcast_fusion), channel_id=1, source_target_pairs={{0,2},{2,0},{4,6},{6,4},{8,10},{10,8},{12,14},{14,12},{1,3},{3,1},... | collective-permute-start | bytes 1671176 | tf_op jit(solution)/shard_map/ppermute | solution.py:322
  127.5 27.6 %all-to-all-start.4 = ((bf16[16,1,8,2048]{3,2,1,0:T(8,128)(2,1)}), bf16[16,1,8,2048]{3,2,1,0:T(8,128)(2,1)S(1)}, u32[]{:S(2)}, u32[]{:S(2)}) async-start(bf16[16,1,8,2048]{3,2,1,0:T(8,128)(2,1)} %get-tuple-element.23), calls=%async_computation.4 | async-start | bytes 1048576 | tf_op jit(solution)/shard_map/all_to_all | solution.py:361
  145.4 9.6 %collective-permute-start.2 = (bf16[2,32,2176]{2,1,0:T(8,128)(2,1)S(1)}, bf16[2,32,2176]{2,1,0:T(8,128)(2,1)S(1)}, u32[]{:S(2)}, u32[]{:S(2)}) collective-permute-start(bf16[2,32,2176]{2,1,0:T(8,128)(2,1)S(1)} %fusion.5), channel_id=1, source_target_pairs={{0,4},{2,6},{4,0},{6,2},{8,12},{10,14},{12,8},{14,10},{1,5},{3,7},... | collective-permute-start | bytes 835592 | tf_op jit(solution)/shard_map/ppermute | solution.py:322
  155.1 8.7 %collective-permute-start.3 = (bf16[1,32,2176]{2,1,0:T(8,128)(2,1)S(1)}, bf16[1,32,2176]{2,1,0:T(8,128)(2,1)S(1)}, u32[]{:S(2)}, u32[]{:S(2)}) collective-permute-start(bf16[1,32,2176]{2,1,0:T(8,128)(2,1)S(1)} %fusion.11), channel_id=1, source_target_pairs={{0,8},{2,10},{4,12},{6,14},{8,0},{10,2},{12,4},{14,6},{1,9},{3,11}... | collective-permute-start | bytes 417800 | tf_op jit(solution)/shard_map/ppermute | solution.py:322
  163.8 1.4 collective-permute-start.4
  164.2 3.2 %copy-start.7 = (bf16[4,8,64,512]{3,2,1,0:T(8,128)(2,1)}, bf16[4,8,64,512]{3,2,1,0:T(8,128)(2,1)S(1)}, u32[]{:S(2)}) copy-start(bf16[4,8,64,512]{3,2,1,0:T(8,128)(2,1)S(1)} %bitcast_dynamic-update-slice_fusion) | copy-start | bytes 6291460

commit v4 on v3

--- a/solution.py
+++ b/solution.py
@@ -14,8 +14,7 @@
 smooth_width = 0.25
 loss_scale = 32.0
 LOG2E = 1.4426950408889634
-TIE_EARLY = 1
-TIE_LATE = 4
+LATE = 3
 
 bf16 = jnp.bfloat16
 f32 = jnp.float32
@@ -56,7 +55,7 @@
         prev_ref, refs = refs[0], refs[1:]
     gx_ref, refs = refs[0], refs[1:]
     if last:
-        mine_ref, sent_ref, refs = refs[0], refs[1], refs[2:]
+        sum_refs, refs = refs[:4], refs[4:]
     else:
         acc_ref, refs = refs[0], refs[1:]
     xf, normed, normed_t, qkv, g_qkv, att, probs, bout, g_pred, g_block, g_att, mask_ref, acc = (
@@ -102,7 +101,7 @@
 
     gain = gain_ref[...]
 
-    @pl.loop(0, members)
+    @pl.loop(0, members, unroll=True)
     def _(m):
         at = pl.ds(pl.multiple_of(m * cells, cells), cells)
         x = xf[at, :]
@@ -114,7 +113,7 @@
     def _():
         fetches[0].wait()
 
-    @pl.loop(0, 3 * width // tile)
+    @pl.loop(0, 3 * width // tile, unroll=True)
     def _(n):
         at = pl.ds(pl.multiple_of(n * tile, tile), tile)
         qkv[:, at] = dot(normed[...], wqkv_ref[:, at]).astype(bf16)
@@ -186,14 +185,14 @@
 
     normed_t[...] = normed[...].T
 
-    @pl.loop(0, 3 * width // tile)
+    @pl.loop(0, 3 * width // tile, unroll=True)
     def _(n):
         at = pl.ds(pl.multiple_of(n * tile, tile), tile)
         acc[:, at] += dot(normed_t[...], g_qkv[:, at])
 
     normed_t[...] = att[...].T
 
-    @pl.loop(0, width // tile)
+    @pl.loop(0, width // tile, unroll=True)
     def _(n):
         at = pl.ds(pl.multiple_of(n * tile, tile), tile)
         there = pl.ds(pl.multiple_of(3 * width + n * tile, tile), tile)
@@ -205,16 +204,17 @@
     def _():
         if last:
             core = lax.axis_index("ens")
-            shards, piece, _ = mine_ref.shape
+            shards, piece, cut = sum_refs[0].shape
             for b in range(shards):
-                low = acc[2 * b * piece : (2 * b + 1) * piece, :]
-                high = acc[(2 * b + 1) * piece : (2 * b + 2) * piece, :]
-                mine_ref[b] = jnp.where(core == 0, low, high).astype(bf16)
-                sent_ref[b] = jnp.where(core == 0, high, low).astype(bf16)
+                for i, span in enumerate((slice(0, cut), slice(cut, acc.shape[1]))):
+                    low = acc[2 * b * piece : (2 * b + 1) * piece, span]
+                    high = acc[(2 * b + 1) * piece : (2 * b + 2) * piece, span]
+                    sum_refs[2 * i][b] = jnp.where(core == 0, low, high).astype(bf16)
+                    sum_refs[2 * i + 1][b] = jnp.where(core == 0, high, low).astype(bf16)
         else:
             pltpu.make_async_copy(acc, acc_ref, sems.at[3]).start()
 
-    @pl.loop(0, width // tile)
+    @pl.loop(0, width // tile, unroll=True)
     def _(n):
         at = pl.ds(pl.multiple_of(n * tile, tile), tile)
         g_att[:, at] = dot_t(g_qkv[...], wqkv_ref[at, :]).astype(bf16)
@@ -270,9 +270,11 @@
     out_specs = [pl.BlockSpec((sources, 1, lat, lanes), lambda i: (0, i, 0, 0))]
     out_shape = [jax.ShapeDtypeStruct((sources, count, lat, lanes), bf16)]
     if shards:
-        sums = (shards, width // shards // 2, total)
-        out_specs += [whole(sums)] * 2
-        out_shape += [jax.ShapeDtypeStruct(sums, bf16)] * 2
+        cut = total // 256 * 128
+        for part in (cut, cut, total - cut, total - cut):
+            sums = (shards, width // shards // 2, part)
+            out_specs.append(whole(sums))
+            out_shape.append(jax.ShapeDtypeStruct(sums, bf16))
     else:
         out_specs.append(anywhere)
         out_shape.append(jax.ShapeDtypeStruct((width, total), f32))
@@ -301,7 +303,7 @@
             pltpu.VMEM(w_head.shape, bf16),
             pltpu.SemaphoreType.DMA((4,)),
         ],
-        compiler_params=pltpu.CompilerParams(vmem_limit_bytes=48 * 1024 * 1024),
+        compiler_params=pltpu.CompilerParams(vmem_limit_bytes=60 * 1024 * 1024),
         cost_estimate=pl.CostEstimate(
             flops=count * 8_000_000_000, bytes_accessed=16_000_000, transcendentals=1_000_000
         ),
@@ -309,39 +311,40 @@
     )(*args)
 
 
-def swap_halves(pair, axes, bit, keep_first):
-    kept = jnp.where(keep_first, pair[0], pair[1])
-    return swap_sum(kept, jnp.where(keep_first, pair[1], pair[0]), axes, bit)
-
-
 def swap_sum(kept, given, axes, bit):
     count = 1
     for axis in axes:
         count *= lax.axis_size(axis)
-    swap = [(i, i ^ bit) for i in range(count)]
-    taken = lax.ppermute(given, axes, swap)
+    taken = lax.ppermute(given, axes, [(i, i ^ bit) for i in range(count)])
     return (kept.astype(f32) + taken.astype(f32)).astype(kept.dtype)
 
 
-def reduce_rows(mine, given, early, late):
+def reduce_rows(sums, early, late):
     lon = ("col", "spread")
     shards = lax.axis_size("col") * lax.axis_size("spread")
+    bits = shards.bit_length() - 1
+    assert shards == 1 << bits
     me = lax.axis_index(lon)
     first = lax.axis_index("ens") == 0
-    rest = swap_sum(mine, given, ("ens",), 1)
-    bit = 1
-    while bit < shards:
-        left = rest.shape[0]
-        pair = rest.reshape(left // 2, 2, *rest.shape[1:]).swapaxes(0, 1)
-        if bit == TIE_EARLY:
-            pair, early = lax.optimization_barrier((pair, early))
-        if bit == TIE_LATE:
-            pair, late = lax.optimization_barrier((pair, late))
-        rest = swap_halves(pair, lon, bit, (me // bit) % 2 == 0)
-        bit *= 2
-    share = rest[0]
-    if TIE_LATE is None:
-        share, late = lax.optimization_barrier((share, late))
+    (*sums, early) = lax.optimization_barrier((*sums, early))
+    rest = [swap_sum(mine, given, ("ens",), 1) for mine, given in sums]
+    rest = [r.reshape((2,) * bits + r.shape[1:]) for r in rest]
+    orders = [list(range(bits)), [1, 0] + list(range(2, bits))]
+    left = [list(range(bits))[::-1] for _ in orders]
+    for i in range(bits):
+        if i == LATE:
+            *rest, late = lax.optimization_barrier((*rest, late))
+        for c, order in enumerate(orders):
+            axis = left[c].index(order[i])
+            left[c].remove(order[i])
+            low, high = (lax.index_in_dim(rest[c], h, axis, keepdims=False) for h in range(2))
+            mine = (me >> order[i]) % 2 == 0
+            rest[c] = swap_sum(
+                jnp.where(mine, low, high), jnp.where(mine, high, low), lon, 1 << order[i]
+            )
+    if LATE >= bits:
+        *rest, late = lax.optimization_barrier((*rest, late))
+    share = jnp.concatenate(rest, axis=-1)
     other = lax.ppermute(share, "ens", [(0, 1), (1, 0)])
     share = jnp.concatenate(
         [jnp.where(first, share, other), jnp.where(first, other, share)], axis=0
@@ -369,30 +372,27 @@
         send_t = target_part[:, span].reshape(lat, count, owners, chans).transpose(2, 1, 0, 3)
         return jnp.concatenate([send_x, send_t], axis=-1)
 
-    lead, main = each // 4, each // 2
-    tail = each - lead - main
+    lead = each // 2
+    tail = each - lead
     x_lead = move(outgoing(0, lead))
-    x_main = move(outgoing(lead, main))
+    x_tail = move(outgoing(lead, tail))
     weights = (gain, w_qkv, w_out, w_head)
     g_lead, acc = block_call(x_lead, *weights, None, 0)
-    both = move(jnp.concatenate([outgoing(lead + main, tail), g_lead], axis=-1))
-    g_main, acc = block_call(x_main, *weights, acc, 0)
-    g_main = move(g_main)
-    g_tail, mine, given = block_call(both, *weights, acc, shards)
+    g_lead = move(g_lead)
+    g_tail, *sums = block_call(x_tail, *weights, acc, shards)
     g_tail = move(g_tail)
-    back_lead = both[..., lanes + chans :]
-    share, (g_main,), g_tail = reduce_rows(mine, given, [g_main], g_tail)
+    share, g_lead, g_tail = reduce_rows((sums[:2], sums[2:]), g_lead, g_tail)
     share = share.astype(f32)
     columns = (
         lambda g: g.reshape(owners, -1, lat, members, width)
         .transpose(3, 2, 1, 0, 4)
         .reshape(members, lat, -1, width)
     )
-    ready = jnp.concatenate([columns(back_lead), columns(g_main)], axis=2)
+    ready = columns(g_lead)
     ready = jnp.pad(ready, ((0, 0), (0, 0), (0, tail * owners), (0, 0)))
     ready = lax.optimization_barrier(ready)
     grad_input = lax.dynamic_update_slice(
-        ready, columns(g_tail), (0, 0, (lead + main) * owners, 0)
+        ready, columns(g_tail), (0, 0, lead * owners, 0)
     )
     grad_qkv = share[:, : 3 * width]
     grad_out = share[:, 3 * width : 4 * width]

time: 168 us -> 149 us (0.89)
  Pallas kernels: 64.8 us -> 50.1 us
  local copies, waits for them, and re-layouts: 11.9 us -> 5.44 us
  waiting for transfers between devices: 44.2 us -> 48 us
  other arithmetic: 8.74 us -> 5.53 us
  starting transfers between devices: 36.8 us -> 38.6 us
    pallas_call x3 -> x2, Pallas kernels: 64.8 us -> 50.1 us  [block_call(): pl.pallas_call(functools.partial(block_kernel, members, width, chans, pre...]
    ppermute x4 -> x8, starting transfers between devices: 6.71 us -> 12.1 us  [swap_sum(): taken = lax.ppermute(given, axes, [(i, i ^ bit) for i in range(count)])]
    unnamed x18 -> x11, local copies, waits for them, and re-layouts: 5.27 us -> 0.03 us
    all_to_all x5 -> x4, waiting for transfers between devices: 17.7 us -> 22.3 us  [body(): lax.all_to_all(g, axes, split_axis=0, concat_axis=0, tiled=True)]
    all_to_all x5 -> x4, starting transfers between devices: 30 us -> 26.4 us  [body(): lax.all_to_all(g, axes, split_axis=0, concat_axis=0, tiled=True)]
    convert_element_type x2 -> x8, other arithmetic: 2.78 us -> 0.74 us  [swap_sum(): return (kept.astype(f32) + taken.astype(f32)).astype(kept.dtype)]
    transpose x4 -> x0, local copies, waits for them, and re-layouts: 1.93 us -> none  [the longest x3 1.92 us: outgoing(): send_x = send_x.transpose(3, 2, 1, 0, 4).reshape(owners, count, lat, lanes)]
    slice x2 -> x1, local copies, waits for them, and re-layouts: 0.01 us -> 1.79 us  [outgoing(): send_x = inputs[:, :, span].reshape(members, lat, count, owners, width)]
  transfers between devices with their start and end apart: 10 -> 13, of which waited for: 7 -> 7; matrix products, arithmetic and copies ran while one was open for 5% -> 3% of each run, Pallas kernels for 39% -> 34%
where the time goes in v4:
time: 149 us
  Pallas kernels  50.1 us (34%)
  waiting for transfers between devices  48 us (32%)
  starting transfers between devices  38.6 us (26%)
  other arithmetic  5.53 us (4%)
  local copies, waits for them, and re-layouts  5.44 us (4%)
    pallas_call x2, Pallas kernels, block_call(): pl.pallas_call(functools.partial(block_kernel, members, width, chans, pre...  50.1 us
    all_to_all x4, starting transfers between devices, body(): lax.all_to_all(g, axes, split_axis=0, concat_axis=0, tiled=True)  26.4 us
    ppermute x8, waiting for transfers between devices, swap_sum(): taken = lax.ppermute(given, axes, [(i, i ^ bit) for i in range(count)])  25.6 us
    all_to_all x4, waiting for transfers between devices, body(): lax.all_to_all(g, axes, split_axis=0, concat_axis=0, tiled=True)  22.3 us
    ppermute x8, starting transfers between devices, swap_sum(): taken = lax.ppermute(given, axes, [(i, i ^ bit) for i in range(count)])  12.1 us
  transfers between devices with their start and end apart: 13, of which 7 were waited for; matrix products, arithmetic and copies ran while one was open for 3% of the time, Pallas kernels for 34%

profile of v4, /device:TPU:0, one launch (start us, length us, event | category | flops | bytes accessed | tf_op | source)
XLA Modules:
  0.0 148.6 jit_solution(2131003114542934458)
XLA Ops:
  0.6 1.0 fusion.3
  1.7 1.8 %fusion.7 = (bf16[4,8,32,512]{3,2,1,0:T(8,128)(2,1)S(1)}, bf16[4,8,32,512]{3,2,1,0:T(8,128)(2,1)S(1)}) fusion(bf16[4,8,64,512]{3,2,1,0:T(8,128)(2,1)} %param.6), kind=kLoop, calls=%fused_computation.34 | loop fusion | bytes 4194304 | tf_op jit(solution)/shard_map/slice | solution.py:370
  3.5 0.6 copy.20
  4.1 1.1 pad_maximum_fusion.1
  5.2 7.4 %all-to-all-start.1 = ((bf16[16,2,8,2176]{3,2,1,0:T(8,128)(2,1)}), bf16[16,2,8,2176]{3,2,1,0:T(8,128)(2,1)S(1)}, u32[]{:S(2)}, u32[]{:S(2)}) async-start(bf16[16,2,8,2176]{3,2,1,0:T(8,128)(2,1)} %pad_maximum_fusion.1), calls=%async_computation.1 | async-start | bytes 2228224 | tf_op jit(solution)/shard_map/all_to_all | solution.py:364
  12.6 0.6 copy.18
  13.2 1.1 pad_maximum_fusion
  14.3 22.3 %all-to-all-done.1.refs_0_ = bf16[16,2,8,2176]{3,2,1,0:T(8,128)(2,1)S(1)} async-done(((bf16[16,2,8,2176]{3,2,1,0:T(8,128)(2,1)}), bf16[16,2,8,2176]{3,2,1,0:T(8,128)(2,1)S(1)}, u32[]{:S(2)}, u32[]{:S(2)}) %all-to-all-start.1) | async-done | bytes 1114144 | tf_op jit(solution)/shard_map/all_to_all | solution.py:364
  36.6 0.0 copy-start.1
  36.6 7.2 %all-to-all-start = ((bf16[16,2,8,2176]{3,2,1,0:T(8,128)(2,1)}), bf16[16,2,8,2176]{3,2,1,0:T(8,128)(2,1)S(1)}, u32[]{:S(2)}, u32[]{:S(2)}) async-start(bf16[16,2,8,2176]{3,2,1,0:T(8,128)(2,1)} %pad_maximum_fusion), calls=%async_computation | async-start | bytes 2228224 | tf_op jit(solution)/shard_map/all_to_all | solution.py:364
  43.8 0.0 copy-done.1
  43.8 25.2 %grid_block.2 = (bf16[16,2,8,2048]{3,2,1,0:T(8,128)(2,1)}, f32[512,2176]{1,0:T(8,128)}) custom-call(bf16[16,2,8,2176]{3,2,1,0:T(8,128)(2,1)} %copy-done.1, f32[1,512]{1,0:T(1,128)} %bitcast.71, bf16[512,1536]{1,0:T(8,128)(2,1)} %refs_2_.3, bf16[512,512]{1,0:T(8,128)(2,1)} %refs_3_.3, bf16[512,128]{1,0:T(8,128)(2,1)} %refs_4_.3), custom_call_target="tpu_custom_call" | custom-call | flops 16000000000 | bytes 16000000 | tf_op jit(solution)/shard_map/grid_block/pallas_call | solution.py:281
  69.0 0.0 all-to-all-done.refs_0_
  69.0 0.0 copy-start.2
  69.0 6.0 %all-to-all-start.2 = ((bf16[16,2,8,2048]{3,2,1,0:T(8,128)(2,1)}), bf16[16,2,8,2048]{3,2,1,0:T(8,128)(2,1)S(1)}, u32[]{:S(2)}, u32[]{:S(2)}) async-start(bf16[16,2,8,2048]{3,2,1,0:T(8,128)(2,1)} %get-tuple-element.24), calls=%async_computation.2 | async-start | bytes 2097152 | tf_op jit(solution)/shard_map/all_to_all | solution.py:364
  75.0 0.0 copy-done.2
  75.1 24.9 %grid_block.3 = (bf16[16,2,8,2048]{3,2,1,0:T(8,128)(2,1)}, bf16[8,32,1024]{2,1,0:T(8,128)(2,1)}, bf16[8,32,1024]{2,1,0:T(8,128)(2,1)}, bf16[8,32,1152]{2,1,0:T(8,128)(2,1)}, bf16[8,32,1152]{2,1,0:T(8,128)(2,1)}) custom-call(bf16[16,2,8,2176]{3,2,1,0:T(8,128)(2,1)} %copy-done.2, f32[1,512]{1,0:T(1,128)} %bitcast.72, bf16[512,1536]{1,0:T(8,128)(2,1)} %refs_2_.3, ...), custom_call_target="tpu_custom_call" | custom-call | flops 16000000000 | bytes 16000000 | tf_op jit(solution)/shard_map/grid_block/pallas_call | solution.py:281
  100.0 0.0 copy-start.4
  100.0 0.0 all-to-all-done.2
  100.0 0.5 collective-permute-start
  100.5 5.8 %all-to-all-start.3 = ((bf16[16,2,8,2048]{3,2,1,0:T(8,128)(2,1)}), bf16[16,2,8,2048]{3,2,1,0:T(8,128)(2,1)S(1)}, u32[]{:S(2)}, u32[]{:S(2)}) async-start(bf16[16,2,8,2048]{3,2,1,0:T(8,128)(2,1)} %get-tuple-element.30), calls=%async_computation.3 | async-start | bytes 2097152 | tf_op jit(solution)/shard_map/all_to_all | solution.py:364
  106.3 0.0 copy-start.3
  106.3 0.5 collective-permute-start.4
  106.7 0.0 collective-permute-done
  106.7 0.0 copy-done.4
  106.7 0.2 add_convert_fusion.1
  107.0 1.7 %collective-permute-start.1 = (bf16[2,2,32,1024]{3,2,0,1:T(8,128)(2,1)S(1)}, bf16[2,2,32,1024]{3,2,0,1:T(8,128)(2,1)S(1)}, u32[]{:S(2)}, u32[]{:S(2)}) collective-permute-start(bf16[2,2,32,1024]{3,2,0,1:T(8,128)(2,1)S(1)} %select_bitcast_fusion.1), channel_id=1, source_target_pairs={{0,2},{2,0},{4,6},{6,4},{8,10},{10,8},{12,14},{14,12},{1,3},{3,1},... | collective-permute-start | bytes 786440 | tf_op jit(solution)/shard_map/ppermute | solution.py:318
  108.8 0.0 collective-permute-done.4
  108.8 0.0 copy-done.3
  108.8 0.1 add_convert_fusion
  109.0 1.8 %collective-permute-start.5 = (bf16[2,2,32,1152]{3,2,0,1:T(8,128)(2,1)S(1)}, bf16[2,2,32,1152]{3,2,0,1:T(8,128)(2,1)S(1)}, u32[]{:S(2)}, u32[]{:S(2)}) collective-permute-start(bf16[2,2,32,1152]{3,2,0,1:T(8,128)(2,1)S(1)} %select_bitcast_fusion), channel_id=1, source_target_pairs={{0,4},{2,6},{4,0},{6,2},{8,12},{10,14},{12,8},{14,10},{1,5},{3,7},... | collective-permute-start | bytes 884744 | tf_op jit(solution)/shard_map/ppermute | solution.py:318
  110.8 12.6 %collective-permute-done.1 = bf16[2,2,32,1024]{3,2,0,1:T(8,128)(2,1)S(1)} collective-permute-done((bf16[2,2,32,1024]{3,2,0,1:T(8,128)(2,1)S(1)}, bf16[2,2,32,1024]{3,2,0,1:T(8,128)(2,1)S(1)}, u32[]{:S(2)}, u32[]{:S(2)}) %collective-permute-start.1) | collective-permute-done | bytes 262176 | tf_op jit(solution)/shard_map/ppermute | solution.py:318
  123.4 0.1 fusion.1
  123.6 1.0 collective-permute-start.2
  124.6 8.4 %collective-permute-done.5 = bf16[2,2,32,1152]{3,2,0,1:T(8,128)(2,1)S(1)} collective-permute-done((bf16[2,2,32,1152]{3,2,0,1:T(8,128)(2,1)S(1)}, bf16[2,2,32,1152]{3,2,0,1:T(8,128)(2,1)S(1)}, u32[]{:S(2)}, u32[]{:S(2)}) %collective-permute-start.5) | collective-permute-done | bytes 294944 | tf_op jit(solution)/shard_map/ppermute | solution.py:318
  133.0 0.1 fusion
  133.2 1.5 %collective-permute-start.6 = (bf16[2,32,1152]{2,1,0:T(8,128)(2,1)S(1)}, bf16[2,32,1152]{2,1,0:T(8,128)(2,1)S(1)}, u32[]{:S(2)}, u32[]{:S(2)}) collective-permute-start(bf16[2,32,1152]{2,1,0:T(8,128)(2,1)S(1)} %select_bitcast_fusion.2), channel_id=1, source_target_pairs={{0,2},{2,0},{4,6},{6,4},{8,10},{10,8},{12,14},{14,12},{1,3},{3,1},... | collective-permute-start | bytes 442376 | tf_op jit(solution)/shard_map/ppermute | solution.py:318
  134.7 0.6 collective-permute-done.2
  135.4 0.1 fusion.4
  135.4 2.6 %collective-permute-start.3 = (bf16[32,1024]{1,0:T(8,128)(2,1)S(1)}, bf16[32,1024]{1,0:T(8,128)(2,1)S(1)}, u32[]{:S(2)}, u32[]{:S(2)}) collective-permute-start(bf16[32,1024]{1,0:T(8,128)(2,1)S(1)} %select_bitcast_fusion.5), channel_id=1, source_target_pairs={{0,8},{2,10},{4,12},{6,14},{8,0},{10,2},{12,4},{14,6},{1,9},{3,11}... | collective-permute-start | bytes 196616 | tf_op jit(solution)/shard_map/ppermute | solution.py:318
  138.0 0.4 collective-permute-done.6
  138.4 0.1 fusion.2
  138.5 2.6 %collective-permute-start.7 = (bf16[32,1152]{1,0:T(8,128)(2,1)S(1)}, bf16[32,1152]{1,0:T(8,128)(2,1)S(1)}, u32[]{:S(2)}, u32[]{:S(2)}) collective-permute-start(bf16[32,1152]{1,0:T(8,128)(2,1)S(1)} %select_bitcast_fusion.4), channel_id=1, source_target_pairs={{0,8},{2,10},{4,12},{6,14},{8,0},{10,2},{12,4},{14,6},{1,9},{3,11}... | collective-permute-start | bytes 221192 | tf_op jit(solution)/shard_map/ppermute | solution.py:318
  141.0 1.6 %collective-permute-done.3 = bf16[32,1024]{1,0:T(8,128)(2,1)S(1)} collective-permute-done((bf16[32,1024]{1,0:T(8,128)(2,1)S(1)}, bf16[32,1024]{1,0:T(8,128)(2,1)S(1)}, u32[]{:S(2)}, u32[]{:S(2)}) %collective-permute-start.3) | collective-permute-done | bytes 65568 | tf_op jit(solution)/shard_map/ppermute | solution.py:318
  142.7 1.9 %collective-permute-done.7 = bf16[32,1152]{1,0:T(8,128)(2,1)S(1)} collective-permute-done((bf16[32,1152]{1,0:T(8,128)(2,1)S(1)}, bf16[32,1152]{1,0:T(8,128)(2,1)S(1)}, u32[]{:S(2)}, u32[]{:S(2)}) %collective-permute-start.7) | collective-permute-done | bytes 73760 | tf_op jit(solution)/shard_map/ppermute | solution.py:318
  144.6 0.0 all-to-all-done.3
  144.7 0.1 collective-permute-start.8
  144.8 0.6 copy.22
  145.3 0.3 pad.4
  145.6 0.6 copy.27
  146.2 0.1 constant_dynamic-update-slice_fusion.2
  146.3 0.0 copy-start
  146.3 0.0 collective-permute-done.8
  146.4 0.8 maximum_convert_fusion.1
  147.2 0.6 maximum_convert_fusion.2
  147.8 0.8 slice.90
  148.6 0.0 copy-done
  (17 shorter events, 0.4 us)
Async XLA Ops:
  5.2 31.4 %all-to-all-start.1 = ((bf16[16,2,8,2176]{3,2,1,0:T(8,128)(2,1)}), bf16[16,2,8,2176]{3,2,1,0:T(8,128)(2,1)S(1)}, u32[]{:S(2)}, u32[]{:S(2)}) async-start(bf16[16,2,8,2176]{3,2,1,0:T(8,128)(2,1)} %pad_maximum_fusion.1), calls=%async_computation.1 | async-start | bytes 2228224 | tf_op jit(solution)/shard_map/all_to_all | solution.py:364
  36.6 7.2 %copy-start.1 = (bf16[16,2,8,2176]{3,2,1,0:T(8,128)(2,1)}, bf16[16,2,8,2176]{3,2,1,0:T(8,128)(2,1)S(1)}, u32[]{:S(2)}) copy-start(bf16[16,2,8,2176]{3,2,1,0:T(8,128)(2,1)S(1)} %all-to-all-done.1.refs_0_) | copy-start | bytes 3342340
  36.6 32.4 %all-to-all-start = ((bf16[16,2,8,2176]{3,2,1,0:T(8,128)(2,1)}), bf16[16,2,8,2176]{3,2,1,0:T(8,128)(2,1)S(1)}, u32[]{:S(2)}, u32[]{:S(2)}) async-start(bf16[16,2,8,2176]{3,2,1,0:T(8,128)(2,1)} %pad_maximum_fusion), calls=%async_computation | async-start | bytes 2228224 | tf_op jit(solution)/shard_map/all_to_all | solution.py:364
  69.0 6.0 %copy-start.2 = (bf16[16,2,8,2176]{3,2,1,0:T(8,128)(2,1)}, bf16[16,2,8,2176]{3,2,1,0:T(8,128)(2,1)S(1)}, u32[]{:S(2)}) copy-start(bf16[16,2,8,2176]{3,2,1,0:T(8,128)(2,1)S(1)} %all-to-all-done.refs_0_) | copy-start | bytes 3342340
  69.0 31.0 %all-to-all-start.2 = ((bf16[16,2,8,2048]{3,2,1,0:T(8,128)(2,1)}), bf16[16,2,8,2048]{3,2,1,0:T(8,128)(2,1)S(1)}, u32[]{:S(2)}, u32[]{:S(2)}) async-start(bf16[16,2,8,2048]{3,2,1,0:T(8,128)(2,1)} %get-tuple-element.24), calls=%async_computation.2 | async-start | bytes 2097152 | tf_op jit(solution)/shard_map/all_to_all | solution.py:364
  100.0 6.7 %copy-start.4 = (bf16[8,32,1024]{2,1,0:T(8,128)(2,1)S(1)}, bf16[8,32,1024]{2,1,0:T(8,128)(2,1)}, u32[]{:S(2)}) copy-start(bf16[8,32,1024]{2,1,0:T(8,128)(2,1)} %get-tuple-element.26) | copy-start | bytes 1572868
  100.0 6.7 %collective-permute-start = (bf16[8,32,1024]{2,1,0:T(8,128)(2,1)}, bf16[8,32,1024]{2,1,0:T(8,128)(2,1)S(1)}, u32[]{:S(2)}, u32[]{:S(2)}) collective-permute-start(bf16[8,32,1024]{2,1,0:T(8,128)(2,1)} %get-tuple-element.27), channel_id=1, source_target_pairs={{0,1},{1,0},{2,3},{3,2},{4,5},{5,4},{6,7},{7,6},{8,9},{9,8},{10,11... | collective-permute-start | bytes 1572872 | tf_op jit(solution)/shard_map/ppermute | solution.py:318
  100.5 44.2 %all-to-all-start.3 = ((bf16[16,2,8,2048]{3,2,1,0:T(8,128)(2,1)}), bf16[16,2,8,2048]{3,2,1,0:T(8,128)(2,1)S(1)}, u32[]{:S(2)}, u32[]{:S(2)}) async-start(bf16[16,2,8,2048]{3,2,1,0:T(8,128)(2,1)} %get-tuple-element.30), calls=%async_computation.3 | async-start | bytes 2097152 | tf_op jit(solution)/shard_map/all_to_all | solution.py:364
  106.3 2.5 %copy-start.3 = (bf16[8,32,1152]{2,1,0:T(8,128)(2,1)S(1)}, bf16[8,32,1152]{2,1,0:T(8,128)(2,1)}, u32[]{:S(2)}) copy-start(bf16[8,32,1152]{2,1,0:T(8,128)(2,1)} %get-tuple-element.28) | copy-start | bytes 1769476
  106.3 2.5 %collective-permute-start.4 = (bf16[8,32,1152]{2,1,0:T(8,128)(2,1)}, bf16[8,32,1152]{2,1,0:T(8,128)(2,1)S(1)}, u32[]{:S(2)}, u32[]{:S(2)}) collective-permute-start(bf16[8,32,1152]{2,1,0:T(8,128)(2,1)} %get-tuple-element.29), channel_id=1, source_target_pairs={{0,1},{1,0},{2,3},{3,2},{4,5},{5,4},{6,7},{7,6},{8,9},{9,8},{10,11... | collective-permute-start | bytes 1769480 | tf_op jit(solution)/shard_map/ppermute | solution.py:318
  107.0 16.4 %collective-permute-start.1 = (bf16[2,2,32,1024]{3,2,0,1:T(8,128)(2,1)S(1)}, bf16[2,2,32,1024]{3,2,0,1:T(8,128)(2,1)S(1)}, u32[]{:S(2)}, u32[]{:S(2)}) collective-permute-start(bf16[2,2,32,1024]{3,2,0,1:T(8,128)(2,1)S(1)} %select_bitcast_fusion.1), channel_id=1, source_target_pairs={{0,2},{2,0},{4,6},{6,4},{8,10},{10,8},{12,14},{14,12},{1,3},{3,1},... | collective-permute-start | bytes 786440 | tf_op jit(solution)/shard_map/ppermute | solution.py:318
  109.0 24.0 %collective-permute-start.5 = (bf16[2,2,32,1152]{3,2,0,1:T(8,128)(2,1)S(1)}, bf16[2,2,32,1152]{3,2,0,1:T(8,128)(2,1)S(1)}, u32[]{:S(2)}, u32[]{:S(2)}) collective-permute-start(bf16[2,2,32,1152]{3,2,0,1:T(8,128)(2,1)S(1)} %select_bitcast_fusion), channel_id=1, source_target_pairs={{0,4},{2,6},{4,0},{6,2},{8,12},{10,14},{12,8},{14,10},{1,5},{3,7},... | collective-permute-start | bytes 884744 | tf_op jit(solution)/shard_map/ppermute | solution.py:318
  123.6 11.8 %collective-permute-start.2 = (bf16[2,32,1024]{2,1,0:T(8,128)(2,1)S(1)}, bf16[2,32,1024]{2,1,0:T(8,128)(2,1)S(1)}, u32[]{:S(2)}, u32[]{:S(2)}) collective-permute-start(bf16[2,32,1024]{2,1,0:T(8,128)(2,1)S(1)} %select_bitcast_fusion.3), channel_id=1, source_target_pairs={{0,4},{2,6},{4,0},{6,2},{8,12},{10,14},{12,8},{14,10},{1,5},{3,7},... | collective-permute-start | bytes 393224 | tf_op jit(solution)/shard_map/ppermute | solution.py:318
  133.2 5.2 %collective-permute-start.6 = (bf16[2,32,1152]{2,1,0:T(8,128)(2,1)S(1)}, bf16[2,32,1152]{2,1,0:T(8,128)(2,1)S(1)}, u32[]{:S(2)}, u32[]{:S(2)}) collective-permute-start(bf16[2,32,1152]{2,1,0:T(8,128)(2,1)S(1)} %select_bitcast_fusion.2), channel_id=1, source_target_pairs={{0,2},{2,0},{4,6},{6,4},{8,10},{10,8},{12,14},{14,12},{1,3},{3,1},... | collective-permute-start | bytes 442376 | tf_op jit(solution)/shard_map/ppermute | solution.py:318
  135.4 7.2 %collective-permute-start.3 = (bf16[32,1024]{1,0:T(8,128)(2,1)S(1)}, bf16[32,1024]{1,0:T(8,128)(2,1)S(1)}, u32[]{:S(2)}, u32[]{:S(2)}) collective-permute-start(bf16[32,1024]{1,0:T(8,128)(2,1)S(1)} %select_bitcast_fusion.5), channel_id=1, source_target_pairs={{0,8},{2,10},{4,12},{6,14},{8,0},{10,2},{12,4},{14,6},{1,9},{3,11}... | collective-permute-start | bytes 196616 | tf_op jit(solution)/shard_map/ppermute | solution.py:318
  138.5 6.1 %collective-permute-start.7 = (bf16[32,1152]{1,0:T(8,128)(2,1)S(1)}, bf16[32,1152]{1,0:T(8,128)(2,1)S(1)}, u32[]{:S(2)}, u32[]{:S(2)}) collective-permute-start(bf16[32,1152]{1,0:T(8,128)(2,1)S(1)} %select_bitcast_fusion.4), channel_id=1, source_target_pairs={{0,8},{2,10},{4,12},{6,14},{8,0},{10,2},{12,4},{14,6},{1,9},{3,11}... | collective-permute-start | bytes 221192 | tf_op jit(solution)/shard_map/ppermute | solution.py:318
  144.7 1.6 %collective-permute-start.8 = (bf16[32,2176]{1,0:T(8,128)(2,1)S(1)}, bf16[32,2176]{1,0:T(8,128)(2,1)S(1)}, u32[]{:S(2)}, u32[]{:S(2)}) collective-permute-start(bf16[32,2176]{1,0:T(8,128)(2,1)S(1)} %constant_dynamic-update-slice_fusion), channel_id=1, source_target_pairs={{0,1},{1,0},{2,3},{3,2},{4,5},{5,4},{6,7},{7,6},{8,9},{9,8},{10,11... | collective-permute-start | bytes 417800 | tf_op jit(solution)/shard_map/ppermute | solution.py:348
  146.3 2.3 %copy-start = (bf16[4,8,64,512]{3,2,1,0:T(8,128)(2,1)}, bf16[4,8,64,512]{3,2,1,0:T(8,128)(2,1)S(1)}, u32[]{:S(2)}) copy-start(bf16[4,8,64,512]{3,2,1,0:T(8,128)(2,1)S(1)} %constant_dynamic-update-slice_fusion.2) | copy-start | bytes 6291460

commit v5 on v4

--- a/solution.py
+++ b/solution.py
@@ -329,7 +329,7 @@
     (*sums, early) = lax.optimization_barrier((*sums, early))
     rest = [swap_sum(mine, given, ("ens",), 1) for mine, given in sums]
     rest = [r.reshape((2,) * bits + r.shape[1:]) for r in rest]
-    orders = [list(range(bits)), [1, 0] + list(range(2, bits))]
+    orders = [list(range(bits))] * 2
     left = [list(range(bits))[::-1] for _ in orders]
     for i in range(bits):
         if i == LATE:

time: 149 us -> 149 us (level)
  transfers between devices with their start and end apart: 13 -> 13, of which waited for: 7 -> 5; matrix products, arithmetic and copies ran while one was open for 3% -> 3% of each run, Pallas kernels for 34% -> 34%
where the time goes in v5:
time: 149 us; the launch traced here: 148 us
  Pallas kernels  50.1 us (34%)
  waiting for transfers between devices  47.8 us (32%)
  starting transfers between devices  38.3 us (26%)
  other arithmetic  5.53 us (4%)
  local copies, waits for them, and re-layouts  5.44 us (4%)
    pallas_call x2, Pallas kernels, block_call(): pl.pallas_call(functools.partial(block_kernel, members, width, chans, pre...  50.1 us
    all_to_all x4, starting transfers between devices, body(): lax.all_to_all(g, axes, split_axis=0, concat_axis=0, tiled=True)  26.4 us
    ppermute x8, waiting for transfers between devices, swap_sum(): taken = lax.ppermute(given, axes, [(i, i ^ bit) for i in range(count)])  25.5 us
    all_to_all x4, waiting for transfers between devices, body(): lax.all_to_all(g, axes, split_axis=0, concat_axis=0, tiled=True)  22.3 us
    ppermute x8, starting transfers between devices, swap_sum(): taken = lax.ppermute(given, axes, [(i, i ^ bit) for i in range(count)])  11.9 us
  transfers between devices with their start and end apart: 13, of which 5 were waited for; matrix products, arithmetic and copies ran while one was open for 3% of the time, Pallas kernels for 34%

profile of v5, /device:TPU:0, one launch (start us, length us, event | category | flops | bytes accessed | tf_op | source)
XLA Modules:
  0.0 148.3 jit_solution(11284671102168872033)
XLA Ops:
  0.6 1.0 fusion.3
  1.7 1.8 %fusion.7 = (bf16[4,8,32,512]{3,2,1,0:T(8,128)(2,1)S(1)}, bf16[4,8,32,512]{3,2,1,0:T(8,128)(2,1)S(1)}) fusion(bf16[4,8,64,512]{3,2,1,0:T(8,128)(2,1)} %param.6), kind=kLoop, calls=%fused_computation.34 | loop fusion | bytes 4194304 | tf_op jit(solution)/shard_map/slice | solution.py:370
  3.5 0.6 copy.20
  4.1 1.1 pad_maximum_fusion.1
  5.2 7.4 %all-to-all-start.1 = ((bf16[16,2,8,2176]{3,2,1,0:T(8,128)(2,1)}), bf16[16,2,8,2176]{3,2,1,0:T(8,128)(2,1)S(1)}, u32[]{:S(2)}, u32[]{:S(2)}) async-start(bf16[16,2,8,2176]{3,2,1,0:T(8,128)(2,1)} %pad_maximum_fusion.1), calls=%async_computation.1 | async-start | bytes 2228224 | tf_op jit(solution)/shard_map/all_to_all | solution.py:364
  12.6 0.6 copy.18
  13.2 1.1 pad_maximum_fusion
  14.3 22.3 %all-to-all-done.1.refs_0_ = bf16[16,2,8,2176]{3,2,1,0:T(8,128)(2,1)S(1)} async-done(((bf16[16,2,8,2176]{3,2,1,0:T(8,128)(2,1)}), bf16[16,2,8,2176]{3,2,1,0:T(8,128)(2,1)S(1)}, u32[]{:S(2)}, u32[]{:S(2)}) %all-to-all-start.1) | async-done | bytes 1114144 | tf_op jit(solution)/shard_map/all_to_all | solution.py:364
  36.6 0.0 copy-start.1
  36.6 7.2 %all-to-all-start = ((bf16[16,2,8,2176]{3,2,1,0:T(8,128)(2,1)}), bf16[16,2,8,2176]{3,2,1,0:T(8,128)(2,1)S(1)}, u32[]{:S(2)}, u32[]{:S(2)}) async-start(bf16[16,2,8,2176]{3,2,1,0:T(8,128)(2,1)} %pad_maximum_fusion), calls=%async_computation | async-start | bytes 2228224 | tf_op jit(solution)/shard_map/all_to_all | solution.py:364
  43.8 0.0 copy-done.1
  43.8 25.2 %grid_block.2 = (bf16[16,2,8,2048]{3,2,1,0:T(8,128)(2,1)}, f32[512,2176]{1,0:T(8,128)}) custom-call(bf16[16,2,8,2176]{3,2,1,0:T(8,128)(2,1)} %copy-done.1, f32[1,512]{1,0:T(1,128)} %bitcast.71, bf16[512,1536]{1,0:T(8,128)(2,1)} %refs_2_.3, bf16[512,512]{1,0:T(8,128)(2,1)} %refs_3_.3, bf16[512,128]{1,0:T(8,128)(2,1)} %refs_4_.3), custom_call_target="tpu_custom_call" | custom-call | flops 16000000000 | bytes 16000000 | tf_op jit(solution)/shard_map/grid_block/pallas_call | solution.py:281
  69.0 0.0 all-to-all-done.refs_0_
  69.0 0.0 copy-start.2
  69.0 6.0 %all-to-all-start.2 = ((bf16[16,2,8,2048]{3,2,1,0:T(8,128)(2,1)}), bf16[16,2,8,2048]{3,2,1,0:T(8,128)(2,1)S(1)}, u32[]{:S(2)}, u32[]{:S(2)}) async-start(bf16[16,2,8,2048]{3,2,1,0:T(8,128)(2,1)} %get-tuple-element.24), calls=%async_computation.2 | async-start | bytes 2097152 | tf_op jit(solution)/shard_map/all_to_all | solution.py:364
  75.0 0.0 copy-done.2
  75.1 24.9 %grid_block.3 = (bf16[16,2,8,2048]{3,2,1,0:T(8,128)(2,1)}, bf16[8,32,1024]{2,1,0:T(8,128)(2,1)}, bf16[8,32,1024]{2,1,0:T(8,128)(2,1)}, bf16[8,32,1152]{2,1,0:T(8,128)(2,1)}, bf16[8,32,1152]{2,1,0:T(8,128)(2,1)}) custom-call(bf16[16,2,8,2176]{3,2,1,0:T(8,128)(2,1)} %copy-done.2, f32[1,512]{1,0:T(1,128)} %bitcast.72, bf16[512,1536]{1,0:T(8,128)(2,1)} %refs_2_.3, ...), custom_call_target="tpu_custom_call" | custom-call | flops 16000000000 | bytes 16000000 | tf_op jit(solution)/shard_map/grid_block/pallas_call | solution.py:281
  100.0 0.0 copy-start.4
  100.0 0.0 all-to-all-done.2
  100.0 0.5 collective-permute-start
  100.5 5.8 %all-to-all-start.3 = ((bf16[16,2,8,2048]{3,2,1,0:T(8,128)(2,1)}), bf16[16,2,8,2048]{3,2,1,0:T(8,128)(2,1)S(1)}, u32[]{:S(2)}, u32[]{:S(2)}) async-start(bf16[16,2,8,2048]{3,2,1,0:T(8,128)(2,1)} %get-tuple-element.30), calls=%async_computation.3 | async-start | bytes 2097152 | tf_op jit(solution)/shard_map/all_to_all | solution.py:364
  106.3 0.0 copy-start.3
  106.3 0.5 collective-permute-start.4
  106.7 0.0 collective-permute-done
  106.7 0.0 copy-done.4
  106.7 0.2 add_convert_fusion.1
  107.0 1.7 %collective-permute-start.1 = (bf16[2,2,32,1024]{3,2,0,1:T(8,128)(2,1)S(1)}, bf16[2,2,32,1024]{3,2,0,1:T(8,128)(2,1)S(1)}, u32[]{:S(2)}, u32[]{:S(2)}) collective-permute-start(bf16[2,2,32,1024]{3,2,0,1:T(8,128)(2,1)S(1)} %select_bitcast_fusion.1), channel_id=1, source_target_pairs={{0,2},{2,0},{4,6},{6,4},{8,10},{10,8},{12,14},{14,12},{1,3},{3,1},... | collective-permute-start | bytes 786440 | tf_op jit(solution)/shard_map/ppermute | solution.py:318
  108.8 0.0 collective-permute-done.4
  108.8 0.0 copy-done.3
  108.8 0.1 add_convert_fusion
  109.0 1.8 %collective-permute-start.5 = (bf16[2,2,32,1152]{3,2,0,1:T(8,128)(2,1)S(1)}, bf16[2,2,32,1152]{3,2,0,1:T(8,128)(2,1)S(1)}, u32[]{:S(2)}, u32[]{:S(2)}) collective-permute-start(bf16[2,2,32,1152]{3,2,0,1:T(8,128)(2,1)S(1)} %select_bitcast_fusion), channel_id=1, source_target_pairs={{0,2},{2,0},{4,6},{6,4},{8,10},{10,8},{12,14},{14,12},{1,3},{3,1},... | collective-permute-start | bytes 884744 | tf_op jit(solution)/shard_map/ppermute | solution.py:318
  110.8 13.1 %collective-permute-done.1 = bf16[2,2,32,1024]{3,2,0,1:T(8,128)(2,1)S(1)} collective-permute-done((bf16[2,2,32,1024]{3,2,0,1:T(8,128)(2,1)S(1)}, bf16[2,2,32,1024]{3,2,0,1:T(8,128)(2,1)S(1)}, u32[]{:S(2)}, u32[]{:S(2)}) %collective-permute-start.1) | collective-permute-done | bytes 262176 | tf_op jit(solution)/shard_map/ppermute | solution.py:318
  123.9 0.1 fusion.1
  124.0 1.1 collective-permute-start.2
  125.2 7.4 %collective-permute-done.5 = bf16[2,2,32,1152]{3,2,0,1:T(8,128)(2,1)S(1)} collective-permute-done((bf16[2,2,32,1152]{3,2,0,1:T(8,128)(2,1)S(1)}, bf16[2,2,32,1152]{3,2,0,1:T(8,128)(2,1)S(1)}, u32[]{:S(2)}, u32[]{:S(2)}) %collective-permute-start.5) | collective-permute-done | bytes 294944 | tf_op jit(solution)/shard_map/ppermute | solution.py:318
  132.5 0.1 fusion
  132.7 1.5 %collective-permute-start.6 = (bf16[2,32,1152]{2,1,0:T(8,128)(2,1)S(1)}, bf16[2,32,1152]{2,1,0:T(8,128)(2,1)S(1)}, u32[]{:S(2)}, u32[]{:S(2)}) collective-permute-start(bf16[2,32,1152]{2,1,0:T(8,128)(2,1)S(1)} %select_bitcast_fusion.2), channel_id=1, source_target_pairs={{0,4},{2,6},{4,0},{6,2},{8,12},{10,14},{12,8},{14,10},{1,5},{3,7},... | collective-permute-start | bytes 442376 | tf_op jit(solution)/shard_map/ppermute | solution.py:318
  134.2 0.0 collective-permute-done.2
  134.2 0.1 fusion.4
  134.3 2.4 %collective-permute-start.3 = (bf16[32,1024]{1,0:T(8,128)(2,1)S(1)}, bf16[32,1024]{1,0:T(8,128)(2,1)S(1)}, u32[]{:S(2)}, u32[]{:S(2)}) collective-permute-start(bf16[32,1024]{1,0:T(8,128)(2,1)S(1)} %select_bitcast_fusion.5), channel_id=1, source_target_pairs={{0,8},{2,10},{4,12},{6,14},{8,0},{10,2},{12,4},{14,6},{1,9},{3,11}... | collective-permute-start | bytes 196616 | tf_op jit(solution)/shard_map/ppermute | solution.py:318
  136.7 2.1 %collective-permute-done.6 = bf16[2,32,1152]{2,1,0:T(8,128)(2,1)S(1)} collective-permute-done((bf16[2,32,1152]{2,1,0:T(8,128)(2,1)S(1)}, bf16[2,32,1152]{2,1,0:T(8,128)(2,1)S(1)}, u32[]{:S(2)}, u32[]{:S(2)}) %collective-permute-start.6) | collective-permute-done | bytes 147488 | tf_op jit(solution)/shard_map/ppermute | solution.py:318
  138.9 0.1 fusion.2
  139.0 2.4 %collective-permute-start.7 = (bf16[32,1152]{1,0:T(8,128)(2,1)S(1)}, bf16[32,1152]{1,0:T(8,128)(2,1)S(1)}, u32[]{:S(2)}, u32[]{:S(2)}) collective-permute-start(bf16[32,1152]{1,0:T(8,128)(2,1)S(1)} %select_bitcast_fusion.4), channel_id=1, source_target_pairs={{0,8},{2,10},{4,12},{6,14},{8,0},{10,2},{12,4},{14,6},{1,9},{3,11}... | collective-permute-start | bytes 221192 | tf_op jit(solution)/shard_map/ppermute | solution.py:318
  141.4 0.0 collective-permute-done.3
  141.4 2.9 %collective-permute-done.7 = bf16[32,1152]{1,0:T(8,128)(2,1)S(1)} collective-permute-done((bf16[32,1152]{1,0:T(8,128)(2,1)S(1)}, bf16[32,1152]{1,0:T(8,128)(2,1)S(1)}, u32[]{:S(2)}, u32[]{:S(2)}) %collective-permute-start.7) | collective-permute-done | bytes 73760 | tf_op jit(solution)/shard_map/ppermute | solution.py:318
  144.3 0.0 all-to-all-done.3
  144.3 0.1 collective-permute-start.8
  144.4 0.6 copy.22
  145.0 0.3 pad.4
  145.3 0.6 copy.27
  145.9 0.1 constant_dynamic-update-slice_fusion.2
  146.0 0.0 copy-start
  146.0 0.0 collective-permute-done.8
  146.1 0.8 maximum_convert_fusion.1
  146.9 0.6 maximum_convert_fusion.2
  147.5 0.8 slice.90
  148.3 0.0 copy-done
  (17 shorter events, 0.4 us)
Async XLA Ops:
  5.2 31.4 %all-to-all-start.1 = ((bf16[16,2,8,2176]{3,2,1,0:T(8,128)(2,1)}), bf16[16,2,8,2176]{3,2,1,0:T(8,128)(2,1)S(1)}, u32[]{:S(2)}, u32[]{:S(2)}) async-start(bf16[16,2,8,2176]{3,2,1,0:T(8,128)(2,1)} %pad_maximum_fusion.1), calls=%async_computation.1 | async-start | bytes 2228224 | tf_op jit(solution)/shard_map/all_to_all | solution.py:364
  36.6 7.2 %copy-start.1 = (bf16[16,2,8,2176]{3,2,1,0:T(8,128)(2,1)}, bf16[16,2,8,2176]{3,2,1,0:T(8,128)(2,1)S(1)}, u32[]{:S(2)}) copy-start(bf16[16,2,8,2176]{3,2,1,0:T(8,128)(2,1)S(1)} %all-to-all-done.1.refs_0_) | copy-start | bytes 3342340
  36.6 32.4 %all-to-all-start = ((bf16[16,2,8,2176]{3,2,1,0:T(8,128)(2,1)}), bf16[16,2,8,2176]{3,2,1,0:T(8,128)(2,1)S(1)}, u32[]{:S(2)}, u32[]{:S(2)}) async-start(bf16[16,2,8,2176]{3,2,1,0:T(8,128)(2,1)} %pad_maximum_fusion), calls=%async_computation | async-start | bytes 2228224 | tf_op jit(solution)/shard_map/all_to_all | solution.py:364
  69.0 6.0 %copy-start.2 = (bf16[16,2,8,2176]{3,2,1,0:T(8,128)(2,1)}, bf16[16,2,8,2176]{3,2,1,0:T(8,128)(2,1)S(1)}, u32[]{:S(2)}) copy-start(bf16[16,2,8,2176]{3,2,1,0:T(8,128)(2,1)S(1)} %all-to-all-done.refs_0_) | copy-start | bytes 3342340
  69.0 31.0 %all-to-all-start.2 = ((bf16[16,2,8,2048]{3,2,1,0:T(8,128)(2,1)}), bf16[16,2,8,2048]{3,2,1,0:T(8,128)(2,1)S(1)}, u32[]{:S(2)}, u32[]{:S(2)}) async-start(bf16[16,2,8,2048]{3,2,1,0:T(8,128)(2,1)} %get-tuple-element.24), calls=%async_computation.2 | async-start | bytes 2097152 | tf_op jit(solution)/shard_map/all_to_all | solution.py:364
  100.0 6.7 %copy-start.4 = (bf16[8,32,1024]{2,1,0:T(8,128)(2,1)S(1)}, bf16[8,32,1024]{2,1,0:T(8,128)(2,1)}, u32[]{:S(2)}) copy-start(bf16[8,32,1024]{2,1,0:T(8,128)(2,1)} %get-tuple-element.26) | copy-start | bytes 1572868
  100.0 6.7 %collective-permute-start = (bf16[8,32,1024]{2,1,0:T(8,128)(2,1)}, bf16[8,32,1024]{2,1,0:T(8,128)(2,1)S(1)}, u32[]{:S(2)}, u32[]{:S(2)}) collective-permute-start(bf16[8,32,1024]{2,1,0:T(8,128)(2,1)} %get-tuple-element.27), channel_id=1, source_target_pairs={{0,1},{1,0},{2,3},{3,2},{4,5},{5,4},{6,7},{7,6},{8,9},{9,8},{10,11... | collective-permute-start | bytes 1572872 | tf_op jit(solution)/shard_map/ppermute | solution.py:318
  100.5 43.8 %all-to-all-start.3 = ((bf16[16,2,8,2048]{3,2,1,0:T(8,128)(2,1)}), bf16[16,2,8,2048]{3,2,1,0:T(8,128)(2,1)S(1)}, u32[]{:S(2)}, u32[]{:S(2)}) async-start(bf16[16,2,8,2048]{3,2,1,0:T(8,128)(2,1)} %get-tuple-element.30), calls=%async_computation.3 | async-start | bytes 2097152 | tf_op jit(solution)/shard_map/all_to_all | solution.py:364
  106.3 2.5 %copy-start.3 = (bf16[8,32,1152]{2,1,0:T(8,128)(2,1)S(1)}, bf16[8,32,1152]{2,1,0:T(8,128)(2,1)}, u32[]{:S(2)}) copy-start(bf16[8,32,1152]{2,1,0:T(8,128)(2,1)} %get-tuple-element.28) | copy-start | bytes 1769476
  106.3 2.5 %collective-permute-start.4 = (bf16[8,32,1152]{2,1,0:T(8,128)(2,1)}, bf16[8,32,1152]{2,1,0:T(8,128)(2,1)S(1)}, u32[]{:S(2)}, u32[]{:S(2)}) collective-permute-start(bf16[8,32,1152]{2,1,0:T(8,128)(2,1)} %get-tuple-element.29), channel_id=1, source_target_pairs={{0,1},{1,0},{2,3},{3,2},{4,5},{5,4},{6,7},{7,6},{8,9},{9,8},{10,11... | collective-permute-start | bytes 1769480 | tf_op jit(solution)/shard_map/ppermute | solution.py:318
  107.0 16.9 %collective-permute-start.1 = (bf16[2,2,32,1024]{3,2,0,1:T(8,128)(2,1)S(1)}, bf16[2,2,32,1024]{3,2,0,1:T(8,128)(2,1)S(1)}, u32[]{:S(2)}, u32[]{:S(2)}) collective-permute-start(bf16[2,2,32,1024]{3,2,0,1:T(8,128)(2,1)S(1)} %select_bitcast_fusion.1), channel_id=1, source_target_pairs={{0,2},{2,0},{4,6},{6,4},{8,10},{10,8},{12,14},{14,12},{1,3},{3,1},... | collective-permute-start | bytes 786440 | tf_op jit(solution)/shard_map/ppermute | solution.py:318
  109.0 23.5 %collective-permute-start.5 = (bf16[2,2,32,1152]{3,2,0,1:T(8,128)(2,1)S(1)}, bf16[2,2,32,1152]{3,2,0,1:T(8,128)(2,1)S(1)}, u32[]{:S(2)}, u32[]{:S(2)}) collective-permute-start(bf16[2,2,32,1152]{3,2,0,1:T(8,128)(2,1)S(1)} %select_bitcast_fusion), channel_id=1, source_target_pairs={{0,2},{2,0},{4,6},{6,4},{8,10},{10,8},{12,14},{14,12},{1,3},{3,1},... | collective-permute-start | bytes 884744 | tf_op jit(solution)/shard_map/ppermute | solution.py:318
  124.0 10.2 %collective-permute-start.2 = (bf16[2,32,1024]{2,1,0:T(8,128)(2,1)S(1)}, bf16[2,32,1024]{2,1,0:T(8,128)(2,1)S(1)}, u32[]{:S(2)}, u32[]{:S(2)}) collective-permute-start(bf16[2,32,1024]{2,1,0:T(8,128)(2,1)S(1)} %select_bitcast_fusion.3), channel_id=1, source_target_pairs={{0,4},{2,6},{4,0},{6,2},{8,12},{10,14},{12,8},{14,10},{1,5},{3,7},... | collective-permute-start | bytes 393224 | tf_op jit(solution)/shard_map/ppermute | solution.py:318
  132.7 6.2 %collective-permute-start.6 = (bf16[2,32,1152]{2,1,0:T(8,128)(2,1)S(1)}, bf16[2,32,1152]{2,1,0:T(8,128)(2,1)S(1)}, u32[]{:S(2)}, u32[]{:S(2)}) collective-permute-start(bf16[2,32,1152]{2,1,0:T(8,128)(2,1)S(1)} %select_bitcast_fusion.2), channel_id=1, source_target_pairs={{0,4},{2,6},{4,0},{6,2},{8,12},{10,14},{12,8},{14,10},{1,5},{3,7},... | collective-permute-start | bytes 442376 | tf_op jit(solution)/shard_map/ppermute | solution.py:318
  134.3 7.1 %collective-permute-start.3 = (bf16[32,1024]{1,0:T(8,128)(2,1)S(1)}, bf16[32,1024]{1,0:T(8,128)(2,1)S(1)}, u32[]{:S(2)}, u32[]{:S(2)}) collective-permute-start(bf16[32,1024]{1,0:T(8,128)(2,1)S(1)} %select_bitcast_fusion.5), channel_id=1, source_target_pairs={{0,8},{2,10},{4,12},{6,14},{8,0},{10,2},{12,4},{14,6},{1,9},{3,11}... | collective-permute-start | bytes 196616 | tf_op jit(solution)/shard_map/ppermute | solution.py:318
  139.0 5.3 %collective-permute-start.7 = (bf16[32,1152]{1,0:T(8,128)(2,1)S(1)}, bf16[32,1152]{1,0:T(8,128)(2,1)S(1)}, u32[]{:S(2)}, u32[]{:S(2)}) collective-permute-start(bf16[32,1152]{1,0:T(8,128)(2,1)S(1)} %select_bitcast_fusion.4), channel_id=1, source_target_pairs={{0,8},{2,10},{4,12},{6,14},{8,0},{10,2},{12,4},{14,6},{1,9},{3,11}... | collective-permute-start | bytes 221192 | tf_op jit(solution)/shard_map/ppermute | solution.py:318
  144.3 1.6 %collective-permute-start.8 = (bf16[32,2176]{1,0:T(8,128)(2,1)S(1)}, bf16[32,2176]{1,0:T(8,128)(2,1)S(1)}, u32[]{:S(2)}, u32[]{:S(2)}) collective-permute-start(bf16[32,2176]{1,0:T(8,128)(2,1)S(1)} %constant_dynamic-update-slice_fusion), channel_id=1, source_target_pairs={{0,1},{1,0},{2,3},{3,2},{4,5},{5,4},{6,7},{7,6},{8,9},{9,8},{10,11... | collective-permute-start | bytes 417800 | tf_op jit(solution)/shard_map/ppermute | solution.py:348
  146.0 2.3 %copy-start = (bf16[4,8,64,512]{3,2,1,0:T(8,128)(2,1)}, bf16[4,8,64,512]{3,2,1,0:T(8,128)(2,1)S(1)}, u32[]{:S(2)}) copy-start(bf16[4,8,64,512]{3,2,1,0:T(8,128)(2,1)S(1)} %constant_dynamic-update-slice_fusion.2) | copy-start | bytes 6291460
